TPU v7x, 256 devices: a whole 4x4x8 slice. The times are simulated.
256 devices in a mesh: dp: 32 (over y, z_lo, core), tensor: 8 (over z_hi, x).
Axes of the slice: x: 4, y: 4, z: 8 (z_hi: 2, z_lo: 4; z = z_hi * 4 + z_lo), core: 2. Of those that a mesh axis runs over, the one named last changes fastest.
Arguments:
- input_rows: bfloat16 [16384, 16384], P('dp', 'tensor'), may hold values from -6 to 6
- frozen_projection_output: bfloat16 [16384, 18432], P('dp', 'tensor'), may hold values from -100 to 100
- output_gradient: bfloat16 [16384, 16384], P('dp', 'tensor'), may hold values from -0.29882812 to 0.29882812
- segments: int32 [32, 512], P('dp'), may hold values from 0 to 7, never falling along the last dimension, each value on 1 to 128 neighbouring positions
- adapter_of_group: int32 [32, 1], replicated, may hold values from 0 to 7
- adapter_down_weight: bfloat16 [8, 48, 16384], P(None, None, 'tensor'), may hold values from -0.21875 to 0.21875
- adapter_up_weight: bfloat16 [8, 16, 18432], P(None, None, 'tensor'), may hold values from -0.19921875 to 0.19921875
Outputs:
- grad_down: float32 [8, 48, 16384], P(None, None, 'tensor')
- grad_up: float32 [8, 16, 18432], P(None, None, 'tensor')
Inputs may be any that keep to these rules, and one draw needn't show every extreme that they name: `segments`: ids never fall along a group's tokens; a document holds at most 128 tokens. `adapter_of_group`: every adapter is trained by at least one data group.
All inputs are finite; a program needn't handle non-finite values.
Results may differ from a plain program's by a relative error of at most 0.03.
Values may be sent and summed in bfloat16 or wider, within the bound.
A program may use at most 128 MiB of HBM per device.

v0:
```python
import jax
import jax.numpy as jnp
from jax import lax
from jax.sharding import PartitionSpec as P

HEAD_SIZE = 128
ADAPTER_RANK = 16
QUERY_PER_KEY = 16


adapter_scale = 0.5
masked_score = -1e30


def head_sweep(query_rows, grad_rows, key_rows, value_rows, allowed):
    head_count = query_rows.shape[0]
    sequence_length = key_rows.shape[0]
    block_heads = 4
    scaling = key_rows.shape[-1] ** (-0.5)

    def block_step(totals, inputs):
        queries, head_gradients = inputs
        scores = (
            jnp.einsum("hqd,kd->hqk", queries, key_rows, preferred_element_type=jnp.float32)
            * scaling
        )
        scores = jnp.where(allowed[None], scores, masked_score)
        row_max = jnp.max(scores, axis=-1, keepdims=True)
        weights = jnp.exp(scores - row_max)
        probs = weights / jnp.sum(weights, axis=-1, keepdims=True)
        probs_low = probs.astype(jnp.bfloat16)
        value_gradient = totals[1] + jnp.einsum(
            "hqk,hqd->kd", probs_low, head_gradients, preferred_element_type=jnp.float32
        )
        prob_grad = jnp.einsum(
            "hqd,kd->hqk", head_gradients, value_rows, preferred_element_type=jnp.float32
        )
        row_dot = jnp.sum(probs * prob_grad, axis=-1, keepdims=True)
        score_grad = (probs * (prob_grad - row_dot) * scaling).astype(jnp.bfloat16)
        query_gradient = jnp.einsum(
            "hqk,kd->hqd", score_grad, key_rows, preferred_element_type=jnp.float32
        )
        key_gradient = totals[0] + jnp.einsum(
            "hqk,hqd->kd", score_grad, queries, preferred_element_type=jnp.float32
        )
        return ((key_gradient, value_gradient), query_gradient)

    zeros_kv = jnp.zeros(key_rows.shape, jnp.float32)
    stacked = (
        query_rows.reshape(head_count // block_heads, block_heads, sequence_length, -1),
        grad_rows.reshape(head_count // block_heads, block_heads, sequence_length, -1),
    )
    (key_gradient, value_gradient), query_gradient = lax.scan(
        block_step, (zeros_kv, zeros_kv), stacked
    )
    return (query_gradient.reshape(head_count, sequence_length, -1), key_gradient, value_gradient)


def per_device(
    input_rows,
    frozen_projection_output,
    output_gradient,
    segments,
    adapter_of_group,
    adapter_down_weight,
    adapter_up_weight,
):
    sequence_length = input_rows.shape[0]
    adapter_ids = adapter_of_group[:, 0]
    number_adapters = adapter_down_weight.shape[0]
    matching_adapter = adapter_ids[lax.axis_index("dp")]
    down_mapping = adapter_down_weight[matching_adapter]
    up_mapping = adapter_up_weight[matching_adapter]
    partial_low = lax.dot_general(
        down_mapping, input_rows, (((1,), (1,)), ((), ())), preferred_element_type=jnp.float32
    )
    low_rank = lax.psum(partial_low.astype(jnp.bfloat16), "tensor")
    kv_local = frozen_projection_output.shape[1] // ((QUERY_PER_KEY + 2) * HEAD_SIZE)
    frozen_columns = frozen_projection_output.reshape(
        sequence_length, kv_local, QUERY_PER_KEY + 2, HEAD_SIZE
    )
    upward_columns = up_mapping.reshape(ADAPTER_RANK, kv_local, QUERY_PER_KEY + 2, HEAD_SIZE)
    reduced_query = low_rank[:ADAPTER_RANK]
    reduced_key = low_rank[ADAPTER_RANK : 2 * ADAPTER_RANK]
    reduced_value = low_rank[2 * ADAPTER_RANK :]
    full_queries = (
        frozen_columns[:, :, :QUERY_PER_KEY].astype(jnp.float32)
        + adapter_scale
        * jnp.einsum(
            "oc,oqum->cqum",
            reduced_query,
            upward_columns[:, :, :QUERY_PER_KEY],
            preferred_element_type=jnp.float32,
        )
    ).astype(jnp.bfloat16)
    full_keys = (
        frozen_columns[:, :, QUERY_PER_KEY].astype(jnp.float32)
        + adapter_scale
        * jnp.einsum(
            "qv,qaj->vaj",
            reduced_key,
            upward_columns[:, :, QUERY_PER_KEY],
            preferred_element_type=jnp.float32,
        )
    ).astype(jnp.bfloat16)
    full_values = (
        frozen_columns[:, :, QUERY_PER_KEY + 1].astype(jnp.float32)
        + adapter_scale
        * jnp.einsum(
            "qv,qaj->vaj",
            reduced_value,
            upward_columns[:, :, QUERY_PER_KEY + 1],
            preferred_element_type=jnp.float32,
        )
    ).astype(jnp.bfloat16)
    position = jnp.arange(sequence_length)
    seg_ids = segments[0]
    allowed = (position[:, None] >= position[None, :]) & (seg_ids[:, None] == seg_ids[None, :])
    head_gradients = output_gradient.reshape(sequence_length, kv_local, QUERY_PER_KEY, HEAD_SIZE)
    query_gradient, key_gradient, value_gradient = head_sweep(
        jnp.transpose(full_queries[:, 0], (1, 0, 2)),
        jnp.transpose(head_gradients[:, 0], (1, 0, 2)),
        full_keys[:, 0],
        full_values[:, 0],
        allowed,
    )
    query_list = [query_gradient]
    key_list = [key_gradient]
    value_list = [value_gradient]
    query_grads = jnp.stack(query_list).astype(jnp.bfloat16)
    key_grads = jnp.stack(key_list).astype(jnp.bfloat16)
    value_grads = jnp.stack(value_list).astype(jnp.bfloat16)
    query_up_weight = adapter_scale * jnp.einsum(
        "py,fiym->pfim", reduced_query, query_grads, preferred_element_type=jnp.float32
    )
    key_up_weight = adapter_scale * jnp.einsum(
        "io,hoy->ihy", reduced_key, key_grads, preferred_element_type=jnp.float32
    )
    value_up_weight = adapter_scale * jnp.einsum(
        "io,hoy->ihy", reduced_value, value_grads, preferred_element_type=jnp.float32
    )
    grad_up_local = jnp.concatenate(
        [query_up_weight, key_up_weight[:, :, None], value_up_weight[:, :, None]], axis=2
    ).reshape(ADAPTER_RANK, -1)
    reduced_query_gradient = adapter_scale * jnp.einsum(
        "noxe,oxwe->nw",
        upward_columns[:, :, :QUERY_PER_KEY],
        query_grads,
        preferred_element_type=jnp.float32,
    )
    reduced_key_gradient = adapter_scale * jnp.einsum(
        "qjl,jnl->qn",
        upward_columns[:, :, QUERY_PER_KEY],
        key_grads,
        preferred_element_type=jnp.float32,
    )
    reduced_value_gradient = adapter_scale * jnp.einsum(
        "qjl,jnl->qn",
        upward_columns[:, :, QUERY_PER_KEY + 1],
        value_grads,
        preferred_element_type=jnp.float32,
    )
    partial_grad = jnp.concatenate(
        [reduced_query_gradient, reduced_key_gradient, reduced_value_gradient], axis=0
    )
    low_grad = lax.psum(partial_grad.astype(jnp.bfloat16), "tensor")
    grad_down_local = jnp.dot(low_grad, input_rows, preferred_element_type=jnp.float32)
    owner = (jnp.arange(number_adapters) == matching_adapter).astype(jnp.float32)
    table_down = owner[:, None, None] * grad_down_local[None]
    table_up = owner[:, None, None] * grad_up_local[None]
    grad_down, grad_up = (
        lax.psum(table_down.astype(jnp.bfloat16), "dp").astype(jnp.float32),
        lax.psum(table_up.astype(jnp.bfloat16), "dp").astype(jnp.float32),
    )
    return (grad_down, grad_up)


def solution(mesh):
    placed = (
        P("dp", "tensor"),
        P("dp", "tensor"),
        P("dp", "tensor"),
        P("dp", None),
        P(),
        P(None, None, "tensor"),
        P(None, None, "tensor"),
    )
    return jax.shard_map(
        per_device,
        mesh=mesh,
        in_specs=placed,
        out_specs=(P(None, None, "tensor"), P(None, None, "tensor")),
        check_vma=False,
    )
```

profile of v0, /device:TPU:1, one launch (start us, length us, event | category | flops | bytes accessed | tf_op | source)
XLA Modules:
  0.0 548.9 jit_solution(18111629848119256017)
XLA Ops:
  7.2 1.4 constant_dynamic-slice_fusion.1
  10.5 0.9 constant_dynamic-slice_fusion
  11.5 4.3 copy.21
  15.7 1.0 fusion.95
  16.7 3.1 slice.40
  19.9 0.6 compare_convert_fusion
  20.5 2.5 convolution_convert_fusion
  23.0 49.6 %psum.28 = bf16[48,512]{1,0:T(8,128)(2,1)S(1)} all-reduce(bf16[48,512]{1,0:T(8,128)(2,1)S(1)} %convolution_convert_fusion), channel_id=1, replica_groups=mesh['dp'=32,'tensor'=8] {'tensor'}, use_global_device_ids=true, to_apply=%region_0.0 | all-reduce | flops 24576 | bytes 98304 | tf_op jit(solution)/shard_map/psum | solution.py:77
  72.8 3.9 copy.31
  76.7 1.9 copy_bitcast_fusion
  78.6 0.2 fusion.66
  78.9 0.2 fusion.67
  79.1 2.1 fusion.63
  81.2 118.3 %while.15 = (s32[]{:T(128)}, f32[512,128]{1,0:T(8,128)S(1)}, f32[512,128]{1,0:T(8,128)S(1)}, bf16[4,4,512,128]{3,2,1,0:T(8,128)(2,1)}, bf16[4,4,512,128]{3,2,1,0...) while((s32[]{:T(128)}, f32[512,128]{1,0:T(8,128)S(1)}, ...), condition=%wide.region_5.6_spmd.clone, body=%wide.region_1.5_spmd.clone.sunk | while | flops 1366300160 | bytes 59691636 | solution.py:53
  81.2 1.7 fusion.132
  82.9 0.2 fusion.133
  83.2 4.0 fusion.134
  87.1 3.7 fusion.131
  90.8 9.2 %fusion.137 = bf16[4,4,512,128]{3,2,1,0:T(8,128)(2,1)} fusion(bf16[4,4,512,128]{3,2,1,0:T(8,128)(2,1)} %get-tuple-element.186, s32[]{:T(128)} %get-tuple-element.183, f32[4,512,512]{1,2,0:T(8,128)} %fusion.131, bf16[512,128]{1,0:T(8,128)(2,1)S(1)} %get-tuple-element.199, f32[4,512,512]{1,2,0:T(8,128)} %get-tuple-element.170, ...), kind=kOutput, calls=%fused_computation.20.clone.1 | convolution fusion | flops 275778048 | bytes 17973760 | tf_op jit(solution)/shard_map/while/body/eval_jaxpr/hqk,kd->hqd/dot_general | solution.py:40
  100.0 3.0 fusion.136
  103.1 7.7 %fusion.135 = f32[512,128]{1,0:T(8,128)S(1)} fusion(f32[4,512,512]{1,2,0:T(8,128)} %fusion.131, bf16[4,4,512,128]{3,2,1,0:T(8,128)(2,1)} %get-tuple-element.198, s32[]{:T(128)} %get-tuple-element.183, f32[512,128]{1,0:T(8,128)S(1)} %get-tuple-element.184, pred[]{:T(512)S(6)} %compare.3, f32[4,512,512]{1,2,0:T(8,128)} %get-tuple-element.170, ...), kind=kOutput, calls=%fused_computation.23.clone.1 | convolution fusion | flops 275909120 | bytes 17842688 | tf_op jit(solution)/shard_map/while/body/eval_jaxpr/hqk,hqd->kd/dot_general | solution.py:43
  110.8 1.8 fusion.132
  112.7 4.0 fusion.134
  116.7 3.7 fusion.131
  120.4 9.2 %fusion.137 = bf16[4,4,512,128]{3,2,1,0:T(8,128)(2,1)} fusion(bf16[4,4,512,128]{3,2,1,0:T(8,128)(2,1)} %get-tuple-element.186, s32[]{:T(128)} %get-tuple-element.183, f32[4,512,512]{1,2,0:T(8,128)} %fusion.131, bf16[512,128]{1,0:T(8,128)(2,1)S(1)} %get-tuple-element.199, f32[4,512,512]{1,2,0:T(8,128)} %get-tuple-element.170, ...), kind=kOutput, calls=%fused_computation.20.clone.1 | convolution fusion | flops 275778048 | bytes 17973760 | tf_op jit(solution)/shard_map/while/body/eval_jaxpr/hqk,kd->hqd/dot_general | solution.py:40
  129.6 3.0 fusion.136
  132.7 7.7 %fusion.135 = f32[512,128]{1,0:T(8,128)S(1)} fusion(f32[4,512,512]{1,2,0:T(8,128)} %fusion.131, bf16[4,4,512,128]{3,2,1,0:T(8,128)(2,1)} %get-tuple-element.198, s32[]{:T(128)} %get-tuple-element.183, f32[512,128]{1,0:T(8,128)S(1)} %get-tuple-element.184, pred[]{:T(512)S(6)} %compare.3, f32[4,512,512]{1,2,0:T(8,128)} %get-tuple-element.170, ...), kind=kOutput, calls=%fused_computation.23.clone.1 | convolution fusion | flops 275909120 | bytes 17842688 | tf_op jit(solution)/shard_map/while/body/eval_jaxpr/hqk,hqd->kd/dot_general | solution.py:43
  140.4 1.8 fusion.132
  142.3 4.0 fusion.134
  146.3 3.7 fusion.131
  150.0 9.2 %fusion.137 = bf16[4,4,512,128]{3,2,1,0:T(8,128)(2,1)} fusion(bf16[4,4,512,128]{3,2,1,0:T(8,128)(2,1)} %get-tuple-element.186, s32[]{:T(128)} %get-tuple-element.183, f32[4,512,512]{1,2,0:T(8,128)} %fusion.131, bf16[512,128]{1,0:T(8,128)(2,1)S(1)} %get-tuple-element.199, f32[4,512,512]{1,2,0:T(8,128)} %get-tuple-element.170, ...), kind=kOutput, calls=%fused_computation.20.clone.1 | convolution fusion | flops 275778048 | bytes 17973760 | tf_op jit(solution)/shard_map/while/body/eval_jaxpr/hqk,kd->hqd/dot_general | solution.py:40
  159.2 3.0 fusion.136
  162.2 7.7 %fusion.135 = f32[512,128]{1,0:T(8,128)S(1)} fusion(f32[4,512,512]{1,2,0:T(8,128)} %fusion.131, bf16[4,4,512,128]{3,2,1,0:T(8,128)(2,1)} %get-tuple-element.198, s32[]{:T(128)} %get-tuple-element.183, f32[512,128]{1,0:T(8,128)S(1)} %get-tuple-element.184, pred[]{:T(512)S(6)} %compare.3, f32[4,512,512]{1,2,0:T(8,128)} %get-tuple-element.170, ...), kind=kOutput, calls=%fused_computation.23.clone.1 | convolution fusion | flops 275909120 | bytes 17842688 | tf_op jit(solution)/shard_map/while/body/eval_jaxpr/hqk,hqd->kd/dot_general | solution.py:43
  170.0 1.8 fusion.132
  171.9 4.0 fusion.134
  175.9 3.7 fusion.131
  179.6 9.2 %fusion.137 = bf16[4,4,512,128]{3,2,1,0:T(8,128)(2,1)} fusion(bf16[4,4,512,128]{3,2,1,0:T(8,128)(2,1)} %get-tuple-element.186, s32[]{:T(128)} %get-tuple-element.183, f32[4,512,512]{1,2,0:T(8,128)} %fusion.131, bf16[512,128]{1,0:T(8,128)(2,1)S(1)} %get-tuple-element.199, f32[4,512,512]{1,2,0:T(8,128)} %get-tuple-element.170, ...), kind=kOutput, calls=%fused_computation.20.clone.1 | convolution fusion | flops 275778048 | bytes 17973760 | tf_op jit(solution)/shard_map/while/body/eval_jaxpr/hqk,kd->hqd/dot_general | solution.py:40
  188.8 3.0 fusion.136
  191.8 7.7 %fusion.135 = f32[512,128]{1,0:T(8,128)S(1)} fusion(f32[4,512,512]{1,2,0:T(8,128)} %fusion.131, bf16[4,4,512,128]{3,2,1,0:T(8,128)(2,1)} %get-tuple-element.198, s32[]{:T(128)} %get-tuple-element.183, f32[512,128]{1,0:T(8,128)S(1)} %get-tuple-element.184, pred[]{:T(512)S(6)} %compare.3, f32[4,512,512]{1,2,0:T(8,128)} %get-tuple-element.170, ...), kind=kOutput, calls=%fused_computation.23.clone.1 | convolution fusion | flops 275909120 | bytes 17842688 | tf_op jit(solution)/shard_map/while/body/eval_jaxpr/hqk,hqd->kd/dot_general | solution.py:43
  199.5 2.0 fusion.68
  201.5 2.2 fusion.70
  204.5 39.7 %psum.29 = bf16[48,512]{1,0:T(8,128)(2,1)S(1)} all-reduce(bf16[48,512]{1,0:T(8,128)(2,1)S(1)} %pad_maximum_fusion.1), channel_id=1, replica_groups=mesh['dp'=32,'tensor'=8] {'tensor'}, use_global_device_ids=true, to_apply=%region_6.7 | all-reduce | flops 24576 | bytes 98304 | tf_op jit(solution)/shard_map/psum | solution.py:166
  244.2 2.1 fusion.97
  246.3 1.0 multiply_convert_fusion.2
  247.2 1.5 multiply_convert_fusion.1
  248.7 288.7 %all-reduce.3.cloned.1.call-done = (bf16[8,48,2048]{2,1,0:T(8,128)(2,1)}, bf16[8,16,2304]{2,1,0:T(8,128)(2,1)}) async-done(((bf16[8,48,2048]{2,1,0:T(8,128)(2,1)}, bf16[8,16,2304]{2,1,0:T(8,128)(2,1)}), (bf16[8,48,2048]{2,1,0:T(8,128)(2,1)}, bf16[8,16,2304]{2,1,0:T(8,128)(2,1)})) %all-reduce.3.cloned.1.call-update) | async-done | bytes 2162704 | tf_op jit(solution)/shard_map/psum | solution.py:172
  537.5 3.5 convert_element_type.90
  541.0 1.1 convert_element_type.92
  (29 shorter events, 1.7 us)
Async XLA Ops:
  7.2 69.5 %copy-start = (bf16[512,2048]{1,0:T(8,128)(2,1)S(1)}, bf16[512,2048]{1,0:T(8,128)(2,1)}, u32[]{:S(2)}) copy-start(bf16[512,2048]{1,0:T(8,128)(2,1)} %param.11) | copy-start | bytes 6291460
  7.2 530.3 %all-reduce.3.cloned.1.call-start = ((), (), s32[]{:S(2)}) async-start(), calls=%async_computation | async-start | bytes 4325376 | tf_op jit(solution)/shard_map/psum | solution.py:172
  76.7 2.4 copy-start.1
  76.7 4.5 copy-start.3
  537.5 3.5 copy-start.2
Sparse Core Ops, SparseCore 0:
  248.8 288.5 all-reduce.2
where the time goes:
time: 550 us; the launch traced here: 549 us
  waiting for transfers between devices  289 us (53%)
  matrix products  113 us (21%)
  blocking collectives  89.3 us (16%)
  other arithmetic  24.4 us (4%)
  local copies, waits for them, and re-layouts  17 us (3%)
  between operations  16 us (3%)
    psum x1, waiting for transfers between devices, per_device(): lax.psum(table_down.astype(jnp.bfloat16), 'dp').astype(jnp.float32)  289 us
    psum x1, blocking collectives, per_device(): low_rank = lax.psum(partial_low.astype(jnp.bfloat16), 'tensor')  49.6 us
    psum x1, blocking collectives, per_device(): low_grad = lax.psum(partial_grad.astype(jnp.bfloat16), 'tensor')  39.7 us
    dot_general x4, matrix products, block_step(): jnp.einsum('hqk,kd->hqd', score_grad, key_rows, preferred_element_type=jn...  36.8 us
    dot_general x4, matrix products, block_step(): jnp.einsum('hqk,hqd->kd', score_grad, queries, preferred_element_type=jnp...  30.7 us
    sub x4, other arithmetic, block_step(): weights = jnp.exp(scores - row_max)  15.9 us
    dot_general x4, matrix products, block_step(): jnp.einsum('hqd,kd->hqk', head_gradients, value_rows, preferred_element_t...  14.7 us
    dot_general x4, matrix products, block_step(): jnp.einsum('hqk,hqd->kd', probs_low, head_gradients, preferred_element_ty...  12.2 us
  transfers between devices with their start and end apart: 1, of which 1 were waited for; matrix products, arithmetic and copies ran while one was open for 0% of the time, Pallas kernels for 0%

commit v1 on v0

v1 whole, which is shorter than its diff:
```python
import functools
import math

import jax
import jax.numpy as jnp
from jax import lax
from jax.experimental import pallas as pl
from jax.experimental.pallas import tpu as pltpu
from jax.sharding import PartitionSpec as P

MESH = pl.DeviceIdType.MESH
VMEM = pltpu.VMEM
SMEM = pltpu.SMEM
DMA = pltpu.SemaphoreType.DMA

HEAD = 128
RANK = 16
HEADS = 16
KINDS = 3
BLOCK = 128
N_TENSOR = 8
N_X = 4
N_Y = 4
N_Z = 4
CHIPS = N_Y * N_Z
MEMBERS = 2 * CHIPS
ADAPTERS = 8
STEP_HEADS = 4
masked_score = -1e30

NT = (((1,), (1,)), ((), ()))
TN = (((0,), (0,)), ((), ()))
NN = (((1,), (0,)), ((), ()))


def matmul(a, b, dims=NN):
    return lax.dot_general(a, b, dims, preferred_element_type=jnp.float32)


def vmem():
    return pl.BlockSpec(memory_space=VMEM)


def smem():
    return pl.BlockSpec(memory_space=SMEM)


def greet_tensor(barrier):
    dp, me = lax.axis_index("dp"), lax.axis_index("tensor")
    for d in range(1, N_TENSOR):
        other = (me + d) % N_TENSOR
        pl.semaphore_signal(barrier, inc=1, device_id=(dp, other), device_id_type=MESH)


def tensor_scatter(part, inbox, send, recv):
    dp, me = lax.axis_index("dp"), lax.axis_index("tensor")
    copies = []
    for d in range(1, N_TENSOR):
        other = (me + d) % N_TENSOR
        copies.append(
            pltpu.make_async_remote_copy(
                src_ref=part.at[other % N_X],
                dst_ref=inbox.at[me],
                send_sem=send.at[d - 1],
                recv_sem=recv.at[d - 1],
                device_id=(dp, other),
                device_id_type=MESH,
            )
        )
        copies[-1].start()
    inbox[me] = part[me % N_X]
    return copies


def tensor_reduce(inbox, full):
    me = lax.axis_index("tensor")
    total = inbox[0].astype(jnp.float32)
    for i in range(1, N_TENSOR):
        total = total + inbox[i].astype(jnp.float32)
    full[me % N_X] = total.astype(jnp.bfloat16)


def tensor_gather(full, send, recv):
    dp, me = lax.axis_index("dp"), lax.axis_index("tensor")
    x, high = me % N_X, me // N_X
    copies = []
    for d in range(1, N_X):
        other = high * N_X + (x + d) % N_X
        copies.append(
            pltpu.make_async_remote_copy(
                src_ref=full.at[x],
                dst_ref=full.at[x],
                send_sem=send.at[d - 1],
                recv_sem=recv.at[d - 1],
                device_id=(dp, other),
                device_id_type=MESH,
            )
        )
        copies[-1].start()
    return copies


def wait_all(copies):
    for copy in copies:
        copy.wait()


def project_kernel(ids, x_ref, down_ref, low_ref, part, inbox, full, s1, r1, s2, r2):
    barrier = pltpu.get_barrier_semaphore()
    greet_tensor(barrier)
    adapter = ids[lax.axis_index("dp"), 0]
    down = down_ref[adapter]
    low = matmul(down, x_ref[...], NT)
    for b in range(N_X):
        part[b] = low[:, b * BLOCK : (b + 1) * BLOCK].astype(jnp.bfloat16)
    pl.semaphore_wait(barrier, N_TENSOR - 1)
    wait_all(tensor_scatter(part, inbox, s1, r1))
    tensor_reduce(inbox, full)
    wait_all(tensor_gather(full, s2, r2))
    low_ref[...] = full[...]


def attention_kernel(
    ids, base_ref, grad_ref, seg_ref, low_ref, up_ref, plow_ref, upout_ref,
    kwin, vwin, ktrans, bias, qs, gs, dk_acc, dv_acc, gup_q, plow_q, up_half,
):
    i = pl.program_id(0)
    adapter = ids[lax.axis_index("dp"), 0]
    kcols = pl.ds(HEADS * HEAD, HEAD)
    vcols = pl.ds((HEADS + 1) * HEAD, HEAD)
    scale = 1.0 / math.sqrt(HEAD)

    @pl.when(i == 0)
    def _():
        up_half[...] = (up_ref[adapter].astype(jnp.float32) * 0.5).astype(jnp.bfloat16)
        kwin[BLOCK:] = jnp.zeros((BLOCK, HEAD), jnp.bfloat16)
        vwin[BLOCK:] = jnp.zeros((BLOCK, HEAD), jnp.bfloat16)
        dk_acc[...] = jnp.zeros_like(dk_acc)
        dv_acc[...] = jnp.zeros_like(dv_acc)
        gup_q[...] = jnp.zeros_like(gup_q)

    low_q = low_ref[i, 0:RANK]
    low_k = low_ref[i, RANK : 2 * RANK]
    low_v = low_ref[i, 2 * RANK :]

    kwin[:BLOCK] = kwin[BLOCK:]
    vwin[:BLOCK] = vwin[BLOCK:]
    key = base_ref[:, kcols].astype(jnp.float32) + matmul(low_k, up_half[:, kcols], TN)
    value = base_ref[:, vcols].astype(jnp.float32) + matmul(low_v, up_half[:, vcols], TN)
    kwin[BLOCK:] = key.astype(jnp.bfloat16)
    vwin[BLOCK:] = value.astype(jnp.bfloat16)
    ktrans[...] = kwin[...].astype(jnp.float32).T.astype(jnp.bfloat16)

    now = seg_ref[0, pl.ds(pl.multiple_of(i * BLOCK, BLOCK), BLOCK)]
    before = seg_ref[0, pl.ds(pl.multiple_of(jnp.maximum(i - 1, 0) * BLOCK, BLOCK), BLOCK)]
    here = jnp.broadcast_to(now.astype(jnp.float32)[None, :], (BLOCK, BLOCK))
    old = jnp.broadcast_to(before.astype(jnp.float32)[None, :], (BLOCK, BLOCK))
    old = jnp.where(i == 0, -1.0, old)
    u = lax.broadcasted_iota(jnp.int32, (BLOCK, BLOCK), 0)
    t = lax.broadcasted_iota(jnp.int32, (BLOCK, BLOCK), 1)
    bias[:BLOCK] = jnp.where(old.T == here, 0.0, masked_score)
    bias[BLOCK:] = jnp.where((here.T == here) & (u <= t), 0.0, masked_score)

    plow_q[...] = jnp.zeros_like(plow_q)
    wide = STEP_HEADS * HEAD

    def heads_step(s, carry):
        cols = pl.ds(pl.multiple_of(s * wide, wide), wide)
        up_here = up_half[:, cols]
        q_wide = base_ref[:, cols].astype(jnp.float32) + matmul(low_q, up_here, TN)
        q_wide = q_wide.astype(jnp.bfloat16)
        g_wide = grad_ref[:, cols]
        for h in range(STEP_HEADS):
            qs[h * BLOCK : (h + 1) * BLOCK] = q_wide[:, h * HEAD : (h + 1) * HEAD]
            gs[h * BLOCK : (h + 1) * BLOCK] = g_wide[:, h * HEAD : (h + 1) * HEAD]
        q, g = qs[...], gs[...]
        mask = jnp.concatenate([bias[...]] * STEP_HEADS, axis=1)
        scores = matmul(kwin[...], q, NT) * (scale * math.log2(math.e)) + mask
        top = jnp.max(scores, axis=0, keepdims=True)
        weights = jnp.exp2(scores - top)
        total = jnp.sum(weights, axis=0, keepdims=True)
        probs = weights * (1.0 / total)
        prob_grad = matmul(vwin[...], g, NT)
        row_dot = jnp.sum(probs * prob_grad, axis=0, keepdims=True)
        score_grad = (probs * (prob_grad - row_dot)).astype(jnp.bfloat16)
        rows = pl.ds(pl.multiple_of(i * BLOCK, BLOCK), 2 * BLOCK)
        dv_acc[rows] += matmul(probs.astype(jnp.bfloat16), g)
        dk_acc[rows] += matmul(score_grad, q)
        dq = (matmul(ktrans[...], score_grad) * scale).astype(jnp.bfloat16)
        dq = jnp.concatenate(
            [dq[:, h * BLOCK : (h + 1) * BLOCK] for h in range(STEP_HEADS)], axis=0
        )
        plow_q[...] += matmul(up_here, dq)
        gup_q[:, cols] += matmul(low_q, dq, NT)
        return carry

    lax.fori_loop(0, HEADS // STEP_HEADS, heads_step, 0)
    plow_ref[i, 0:RANK] = plow_q[...].astype(jnp.bfloat16)

    @pl.when(i == pl.num_programs(0) - 1)
    def _():
        dk = (dk_acc[BLOCK:] * scale).astype(jnp.bfloat16)
        dv = dv_acc[BLOCK:].astype(jnp.bfloat16)
        part_k = matmul(up_half[:, kcols], dk, NT)
        part_v = matmul(up_half[:, vcols], dv, NT)
        gup_k = jnp.zeros((RANK, HEAD), jnp.float32)
        gup_v = jnp.zeros((RANK, HEAD), jnp.float32)
        for b in range(4):
            own = slice(b * BLOCK, (b + 1) * BLOCK)
            plow_ref[b, RANK : 2 * RANK] = part_k[:, own].astype(jnp.bfloat16)
            plow_ref[b, 2 * RANK :] = part_v[:, own].astype(jnp.bfloat16)
            gup_k += matmul(low_ref[b, RANK : 2 * RANK], dk[own])
            gup_v += matmul(low_ref[b, 2 * RANK :], dv[own])
        gup_k, gup_v = gup_k * 0.5, gup_v * 0.5
        for j in range(CHIPS):
            upout_ref[j, 0:RANK] = (gup_q[:, j * HEAD : (j + 1) * HEAD] * 0.5).astype(jnp.bfloat16)
            mine = (adapter == j // 2).astype(jnp.float32)
            upout_ref[j, RANK:] = ((gup_v if j % 2 else gup_k) * mine).astype(jnp.bfloat16)


def split_dp():
    dp = lax.axis_index("dp")
    return dp // 2, dp % 2


def scatter(src, inbox, core_to, send, recv):
    dp, tensor = lax.axis_index("dp"), lax.axis_index("tensor")
    chip, core = split_dp()

    def one(k, carry):
        p = (chip + k) % CHIPS
        pltpu.make_async_remote_copy(
            src_ref=src.at[p],
            dst_ref=inbox.at[dp],
            send_sem=send.at[k],
            recv_sem=recv,
            device_id=(2 * p + core_to, tensor),
            device_id_type=MESH,
        ).start()
        return carry

    lax.fori_loop(1, CHIPS, one, 0)

    @pl.when(core == core_to)
    def _():
        pltpu.make_async_copy(src.at[chip], inbox.at[dp], recv).start()

    @pl.when(core != core_to)
    def _():
        one(0, 0)


def scatter_sent(src, inbox, core_to, send, recv):
    dp, tensor = lax.axis_index("dp"), lax.axis_index("tensor")
    chip, core = split_dp()

    def one(k, carry):
        pltpu.make_async_remote_copy(
            src_ref=src.at[chip],
            dst_ref=inbox.at[dp],
            send_sem=send.at[k],
            recv_sem=recv,
            device_id=(2 * chip + core_to, tensor),
            device_id_type=MESH,
        ).wait_send()
        return carry

    lax.fori_loop(1, CHIPS, one, 0)

    @pl.when(core != core_to)
    def _():
        one(0, 0)


def arrived(whole, sem):
    pltpu.make_async_copy(whole, whole, sem).wait()


def sum_adapters(ids, inbox, rows, out, slot):
    def one(m, sums):
        term = inbox[m, rows].astype(jnp.float32)
        adapter = ids[m, 0]
        return tuple(
            sums[a] + term * (adapter == a).astype(jnp.float32) for a in range(ADAPTERS)
        )

    zero = jnp.zeros((rows.stop - rows.start, HEAD), jnp.float32)
    sums = lax.fori_loop(0, MEMBERS, one, (zero,) * ADAPTERS)
    for a in range(ADAPTERS):
        out[slot, a] = sums[a].astype(jnp.bfloat16)


class Stream:
    def __init__(self, out, owner, sems):
        self.out, self.owner = out, owner
        self.zs, self.zr, self.ys, self.yr, self.fs, self.fr, self.cs, self.cr = sems
        self.half = out.shape[1] // 2
        self.tensor = lax.axis_index("tensor")
        self.chip, self.core = split_dp()
        self.y, self.z = self.chip // N_Z, self.chip % N_Z

    def copy(self, slot, chip_to, core_to, send, recv, part=None):
        ref = self.out.at[slot] if part is None else self.out.at[slot, part]
        return pltpu.make_async_remote_copy(
            src_ref=ref,
            dst_ref=ref,
            send_sem=send,
            recv_sem=recv,
            device_id=(2 * chip_to + core_to, self.tensor),
            device_id_type=MESH,
        )

    def at(self, y, z):
        return (y % N_Y) * N_Z + z % N_Z

    def z_copy(self, d):
        return self.copy(
            self.chip, self.at(self.y, self.z + d), self.owner, self.zs.at[d - 1], self.zr.at[d - 1]
        )

    def y_copy(self, dz, side):
        to = self.at(self.y + (1 if side == 0 else 3), self.z)
        slot = self.at(self.y, self.z + N_Z - dz)
        n = 2 * dz + side
        return self.copy(slot, to, self.owner, self.ys.at[n], self.yr.at[n])

    def y_arrival(self, dz, side):
        n = 2 * dz + side
        return self.copy(
            self.y_slot(dz, side), self.chip, self.owner, self.ys.at[n], self.yr.at[n]
        )

    def y_slot(self, dz, side):
        return self.at(self.y + (3 if side == 0 else 1), self.z + N_Z - dz)

    def part(self, side):
        n = self.out.shape[1]
        return pl.ds(0, self.half) if side == 0 else pl.ds(self.half, n - self.half)

    def forward(self, dz, side):
        to = self.at(self.y + (1 if side == 0 else 3), self.z)
        slot = self.y_slot(dz, side)
        n = 2 * dz + side
        return self.copy(slot, to, self.owner, self.fs.at[n], self.fr.at[n], self.part(side))

    def forwarded(self, dz, side):
        slot = self.at(self.y + 2, self.z + N_Z - dz)
        n = 2 * dz + side
        return self.copy(slot, self.chip, self.owner, self.fs.at[n], self.fr.at[n], self.part(side))

    def twin(self, n, slot):
        return self.copy(slot, self.chip, 1 - self.owner, self.cs.at[n], self.cr)

    def start(self):
        for d in (1, 3, 2):
            self.z_copy(d).start()
        for side in range(2):
            self.y_copy(0, side).start()
        self.twin(0, self.chip).start()

    def spread(self):
        for dz in (1, 3, 2):
            self.z_copy(dz).wait_recv()
            for side in range(2):
                self.y_copy(dz, side).start()
            self.twin(dz, self.at(self.y, self.z + N_Z - dz)).start()

    def pass_on(self):
        for dz in (0, 1, 3, 2):
            for side in range(2):
                self.y_arrival(dz, side).wait_recv()
                self.forward(dz, side).start()
                self.twin(4 + 2 * dz + side, self.y_slot(dz, side)).start()

    def finish(self):
        for dz in (0, 1, 3, 2):
            for side in range(2):
                self.forwarded(dz, side).wait_recv()
            self.twin(12 + dz, self.at(self.y + 2, self.z + N_Z - dz)).start()
        for d in range(1, N_Z):
            self.z_copy(d).wait_send()
        for dz in range(N_Z):
            for side in range(2):
                self.y_copy(dz, side).wait_send()
                self.forward(dz, side).wait_send()
        for n in range(CHIPS):
            self.twin(n, self.chip).wait_send()

    def receive(self):
        arrived(self.out, self.cr)


STREAM_SEMS = [DMA((3,)), DMA((3,))] + [DMA((8,))] * 4 + [DMA((CHIPS,)), DMA]


def adapters_kernel(
    ids, x_ref, plow_ref, up_part, out_a, out_b, out_u,
    inbox, full, s1, r1, s2, r2,
    down_a, down_b, in_a, in_b, in_u, sa, sb, su, ra, rb, ru, *sems,
):
    chip, core = split_dp()
    tensor, dp = lax.axis_index("tensor"), lax.axis_index("dp")
    barrier = pltpu.get_barrier_semaphore()
    greet_tensor(barrier)

    def greet(k, carry):
        other = (dp + k) % MEMBERS
        pl.semaphore_signal(barrier, inc=1, device_id=(other, tensor), device_id_type=MESH)
        return carry

    lax.fori_loop(1, MEMBERS, greet, 0)
    pl.semaphore_wait(barrier, N_TENSOR - 1 + MEMBERS - 1)

    stream_a = Stream(out_a, 0, sems[0:8])
    stream_b = Stream(out_b, 1, sems[8:16])
    stream_u = Stream(out_u, 1, sems[16:24])

    copies = tensor_scatter(plow_ref, inbox, s1, r1)
    scatter(up_part, in_u, 1, su, ru)
    wait_all(copies)
    tensor_reduce(inbox, full)
    copies = tensor_gather(full, s2, r2)

    @pl.when(core == 1)
    def _():
        arrived(in_u, ru)
        sum_adapters(ids, in_u, slice(0, RANK), out_u, chip)

        def one(m, total):
            return total + in_u[m, RANK:].astype(jnp.float32)

        total = lax.fori_loop(0, MEMBERS, one, jnp.zeros((RANK, HEAD), jnp.float32))
        out_u[chip, ADAPTERS] = total.astype(jnp.bfloat16)
        stream_u.start()

    wait_all(copies)
    low_grad = jnp.concatenate([full[b] for b in range(N_X)], axis=1)
    step = 4

    def columns(s, carry):
        cols = pl.ds(pl.multiple_of(s * (step * HEAD), step * HEAD), step * HEAD)
        product = matmul(low_grad, x_ref[:, cols]).astype(jnp.bfloat16)
        for j in range(step):
            tile = product[:, j * HEAD : (j + 1) * HEAD]
            down_a[s * step + j] = tile[: 2 * RANK]
            down_b[s * step + j] = tile[2 * RANK :]
        return carry

    lax.fori_loop(0, CHIPS // step, columns, 0)
    scatter(down_a, in_a, 0, sa, ra)
    scatter(down_b, in_b, 1, sb, rb)

    @pl.when(core == 0)
    def _():
        arrived(in_a, ra)
        sum_adapters(ids, in_a, slice(0, 2 * RANK), out_a, chip)
        stream_a.start()
        stream_a.spread()
        stream_a.pass_on()
        stream_a.finish()
        stream_b.receive()
        stream_u.receive()

    @pl.when(core == 1)
    def _():
        stream_u.spread()
        arrived(in_b, rb)
        sum_adapters(ids, in_b, slice(0, RANK), out_b, chip)
        stream_b.start()
        stream_u.pass_on()
        stream_b.spread()
        stream_b.pass_on()
        stream_u.finish()
        stream_b.finish()
        stream_a.receive()

    scatter_sent(up_part, in_u, 1, su, ru)
    scatter_sent(down_a, in_a, 0, sa, ra)
    scatter_sent(down_b, in_b, 1, sb, rb)


def widen_kernel(a_ref, b_ref, u_ref, kv_ref, down_ref, up_ref):
    for j in range(CHIPS):
        cols = slice(j * HEAD, (j + 1) * HEAD)
        down_ref[0, : 2 * RANK, cols] = a_ref[j, 0].astype(jnp.float32)
        down_ref[0, 2 * RANK :, cols] = b_ref[j, 0].astype(jnp.float32)
        up_ref[0, :, cols] = u_ref[j, 0].astype(jnp.float32)
    for kind in range(2):
        cols = slice((CHIPS + kind) * HEAD, (CHIPS + kind + 1) * HEAD)
        up_ref[0, :, cols] = kv_ref[kind, 0].astype(jnp.float32)


def per_device(x, base, grad, segments, ids, down, up):
    bf16, f32 = jnp.bfloat16, jnp.float32
    tokens, width = x.shape
    rows = KINDS * RANK
    blocks = tokens // BLOCK
    limit = 56 * 1024 * 1024

    low = pl.pallas_call(
        project_kernel,
        out_shape=jax.ShapeDtypeStruct((blocks, rows, BLOCK), bf16),
        in_specs=[smem(), vmem(), vmem()],
        out_specs=vmem(),
        scratch_shapes=[
            VMEM((blocks, rows, BLOCK), bf16),
            VMEM((N_TENSOR, rows, BLOCK), bf16),
            VMEM((blocks, rows, BLOCK), bf16),
            DMA((7,)), DMA((7,)), DMA((3,)), DMA((3,)),
        ],
        compiler_params=pltpu.CompilerParams(
            collective_id=0, has_side_effects=True, vmem_limit_bytes=limit
        ),
        name="project",
    )(ids, x, down)

    cols = base.shape[1]
    wide = STEP_HEADS * HEAD
    plow, up_part = pl.pallas_call(
        attention_kernel,
        grid=(blocks,),
        out_shape=(
            jax.ShapeDtypeStruct((blocks, rows, BLOCK), bf16),
            jax.ShapeDtypeStruct((CHIPS, 2 * RANK, HEAD), bf16),
        ),
        in_specs=[
            smem(),
            pl.BlockSpec((BLOCK, cols), lambda i: (i, 0)),
            pl.BlockSpec((BLOCK, HEADS * HEAD), lambda i: (i, 0)),
            vmem(), vmem(), vmem(),
        ],
        out_specs=(vmem(), vmem()),
        scratch_shapes=[
            VMEM((2 * BLOCK, HEAD), bf16),
            VMEM((2 * BLOCK, HEAD), bf16),
            VMEM((HEAD, 2 * BLOCK), bf16),
            VMEM((2 * BLOCK, BLOCK), f32),
            VMEM((wide, HEAD), bf16),
            VMEM((wide, HEAD), bf16),
            VMEM((tokens + BLOCK, HEAD), f32),
            VMEM((tokens + BLOCK, HEAD), f32),
            VMEM((RANK, HEADS * HEAD), f32),
            VMEM((RANK, BLOCK), f32),
            VMEM((RANK, cols), bf16),
        ],
        compiler_params=pltpu.CompilerParams(vmem_limit_bytes=limit),
        name="attention",
    )(ids, base, grad, segments, low, up)

    out_a, out_b, out_u = pl.pallas_call(
        adapters_kernel,
        out_shape=(
            jax.ShapeDtypeStruct((CHIPS, ADAPTERS, 2 * RANK, HEAD), bf16),
            jax.ShapeDtypeStruct((CHIPS, ADAPTERS, RANK, HEAD), bf16),
            jax.ShapeDtypeStruct((CHIPS, ADAPTERS + 1, RANK, HEAD), bf16),
        ),
        in_specs=[smem(), vmem(), vmem(), vmem()],
        out_specs=(vmem(), vmem(), vmem()),
        scratch_shapes=[
            VMEM((N_TENSOR, rows, BLOCK), bf16),
            VMEM((blocks, rows, BLOCK), bf16),
            DMA((7,)), DMA((7,)), DMA((3,)), DMA((3,)),
            VMEM((CHIPS, 2 * RANK, HEAD), bf16),
            VMEM((CHIPS, RANK, HEAD), bf16),
            VMEM((MEMBERS, 2 * RANK, HEAD), bf16),
            VMEM((MEMBERS, RANK, HEAD), bf16),
            VMEM((MEMBERS, 2 * RANK, HEAD), bf16),
            DMA((CHIPS,)), DMA((CHIPS,)), DMA((CHIPS,)),
            DMA, DMA, DMA,
        ] + STREAM_SEMS * 3,
        compiler_params=pltpu.CompilerParams(
            collective_id=1, has_side_effects=True, vmem_limit_bytes=limit
        ),
        name="adapters",
    )(ids, x, plow, up_part)

    return pl.pallas_call(
        widen_kernel,
        grid=(ADAPTERS,),
        out_shape=(
            jax.ShapeDtypeStruct((ADAPTERS, rows, width), f32),
            jax.ShapeDtypeStruct((ADAPTERS, RANK, cols), f32),
        ),
        in_specs=[
            pl.BlockSpec((CHIPS, 1, 2 * RANK, HEAD), lambda a: (0, a, 0, 0)),
            pl.BlockSpec((CHIPS, 1, RANK, HEAD), lambda a: (0, a, 0, 0)),
            pl.BlockSpec((CHIPS, 1, RANK, HEAD), lambda a: (0, a, 0, 0)),
            pl.BlockSpec((2, 1, RANK, HEAD), lambda a: (a, ADAPTERS, 0, 0)),
        ],
        out_specs=(
            pl.BlockSpec((1, rows, width), lambda a: (a, 0, 0)),
            pl.BlockSpec((1, RANK, cols), lambda a: (a, 0, 0)),
        ),
        compiler_params=pltpu.CompilerParams(vmem_limit_bytes=limit),
        name="widen",
    )(out_a, out_b, out_u, out_u)


def solution(mesh):
    placed = (
        P("dp", "tensor"),
        P("dp", "tensor"),
        P("dp", "tensor"),
        P("dp", None),
        P(),
        P(None, None, "tensor"),
        P(None, None, "tensor"),
    )
    return jax.shard_map(
        per_device,
        mesh=mesh,
        in_specs=placed,
        out_specs=(P(None, None, "tensor"), P(None, None, "tensor")),
        check_vma=False,
    )
```

time: 550 us -> 94.8 us (0.17)
  waiting for transfers between devices: 289 us -> 0 us
  matrix products: 113 us -> 0 us
  Pallas kernels: 0 us -> 92.5 us
  blocking collectives: 89.3 us -> 0 us
  other arithmetic: 24.4 us -> 0 us
  local copies, waits for them, and re-layouts: 17 us -> 1.33 us
  between operations: 16 us -> 0.65 us
    psum x1 -> x0, waiting for transfers between devices: 289 us -> none  [per_device(): lax.psum(table_down.astype(jnp.bfloat16), 'dp').astype(jnp.float32)]
    dot_general x31 -> x0, matrix products: 113 us -> none  [the longest x4 36.8 us: block_step(): jnp.einsum('hqk,kd->hqd', score_grad, key_rows, preferred_element_type=jn...]
    pallas_call x0 -> x4, Pallas kernels: none -> 92.5 us  [the longest x1 46.7 us: per_device(): pl.pallas_call(adapters_kernel, out_shape=(jax.ShapeDtypeStruct((CHIPS, A...]
    psum x2 -> x0, blocking collectives: 89.3 us -> none  [the longest x1 49.6 us: per_device(): low_rank = lax.psum(partial_low.astype(jnp.bfloat16), 'tensor')]
    sub x4 -> x0, other arithmetic: 15.9 us -> none  [block_step(): weights = jnp.exp(scores - row_max)]
    convert_element_type x5 -> x0, other arithmetic: 7.63 us -> none  [the longest x1 3.51 us: per_device(): lax.psum(table_down.astype(jnp.bfloat16), 'dp').astype(jnp.float32)]
    unnamed x13 -> x1, local copies, waits for them, and re-layouts: 8.5 us -> 1.33 us
  transfers between devices with their start and end apart: 1 -> 0, of which waited for: 1 -> 0; matrix products, arithmetic and copies ran while one was open for 0% -> 0% of each run, Pallas kernels for 0% -> 0%
where the time goes in v1:
time: 94.8 us; the launch traced here: 94.5 us
  Pallas kernels  92.5 us (98%)
  local copies, waits for them, and re-layouts  1.33 us (1%)
    pallas_call x1, Pallas kernels, per_device(): pl.pallas_call(adapters_kernel, out_shape=(jax.ShapeDtypeStruct((CHIPS, A...  46.7 us
    pallas_call x1, Pallas kernels, per_device(): pl.pallas_call(attention_kernel, grid=(blocks,), out_shape=(jax.ShapeDtyp...  20.9 us
    pallas_call x1, Pallas kernels, per_device(): pl.pallas_call(project_kernel, out_shape=jax.ShapeDtypeStruct((blocks, ro...  18.8 us
    pallas_call x1, Pallas kernels, per_device(): pl.pallas_call(widen_kernel, grid=(ADAPTERS,), out_shape=(jax.ShapeDtypeS...  6.16 us

profile of v1, /device:TPU:1, one launch (start us, length us, event | category | flops | bytes accessed | tf_op | source)
XLA Modules:
  0.0 94.5 jit_solution(749600539580149679)
XLA Ops:
  0.6 1.3 %copy.11.ids = s32[32,1]{1,0:T(8,128)} copy(s32[32,1]{0,1:T(1,128)} %param.11) | data formatting | bytes 256 | tf_op args[4]
  2.0 18.8 %project.1.low_ref = bf16[4,48,128]{2,1,0:T(8,128)(2,1)} custom-call(s32[32,1]{1,0:T(8,128)} %copy.11.ids, bf16[512,2048]{1,0:T(8,128)(2,1)} %x_ref.3, bf16[8,48,2048]{2,1,0:T(8,128)(2,1)} %down_ref.1), custom_call_target="tpu_custom_call" | custom-call | tf_op jit(solution)/shard_map/project/pallas_call | solution.py:500
  20.8 20.9 %attention.1 = (bf16[4,48,128]{2,1,0:T(8,128)(2,1)}, bf16[16,32,128]{2,1,0:T(8,128)(2,1)}) custom-call(s32[32,1]{1,0:T(8,128)} %copy.11.ids, bf16[512,2304]{1,0:T(8,128)(2,1)} %base_ref.1, bf16[512,2048]{1,0:T(8,128)(2,1)} %grad_ref.1, s32[1,512]{1,0:T(1,128)} %seg_ref.1, bf16[4,48,128]{2,1,0:T(8,128)(2,1)} %project.1.low_ref, bf16[8,16,2304]{2,1,0:T(8,128)(2,1)} %up_ref.1), custom_call_target="tpu_custom_call" | custom-call | tf_op jit(solution)/shard_map/attention/pallas_call | solution.py:519
  41.6 46.7 %adapters.1 = (bf16[16,8,32,128]{3,2,1,0:T(8,128)(2,1)}, bf16[16,8,16,128]{3,2,1,0:T(8,128)(2,1)}, bf16[16,9,16,128]{3,2,1,0:T(8,128)(2,1)}) custom-call(s32[32,1]{1,0:T(8,128)} %copy.11.ids, bf16[512,2048]{1,0:T(8,128)(2,1)} %x_ref.3, bf16[4,48,128]{2,1,0:T(8,128)(2,1)} %get-tuple-element.7.plow_ref, bf16[16,32,128]{2,1,0:T(8,128)(2,1)} %get-tuple-element.8.up_part), custom_call_target="tpu_custom_call" | custom-call | tf_op jit(solution)/shard_map/adapters/pallas_call | solution.py:550
  88.3 6.2 %widen.1 = (f32[8,48,2048]{2,1,0:T(8,128)}, f32[8,16,2304]{2,1,0:T(8,128)}) custom-call(bf16[16,8,32,128]{3,2,1,0:T(8,128)(2,1)} %get-tuple-element.9.a_ref, bf16[16,8,16,128]{3,2,1,0:T(8,128)(2,1)} %get-tuple-element.10.b_ref, bf16[16,9,16,128]{3,2,1,0:T(8,128)(2,1)} %get-tuple-element.11.u_ref.kv_ref, bf16[16,9,16,128]{3,2,1,0:T(8,128)(2,1)} %get-tuple-element.11.u_ref.kv_ref), custom_call_target="tpu_custom_call" | custom-call | tf_op jit(solution)/shard_map/widen/pallas_call | solution.py:577

commit v2 on v1

--- a/solution.py
+++ b/solution.py
@@ -25,7 +25,7 @@
 CHIPS = N_Y * N_Z
 MEMBERS = 2 * CHIPS
 ADAPTERS = 8
-STEP_HEADS = 4
+BLOCKS = 4
 masked_score = -1e30
 
 NT = (((1,), (1,)), ((), ()))
@@ -100,122 +100,14 @@
     return copies
 
 
-def wait_all(copies):
+def received(copies):
     for copy in copies:
-        copy.wait()
-
-
-def project_kernel(ids, x_ref, down_ref, low_ref, part, inbox, full, s1, r1, s2, r2):
-    barrier = pltpu.get_barrier_semaphore()
-    greet_tensor(barrier)
-    adapter = ids[lax.axis_index("dp"), 0]
-    down = down_ref[adapter]
-    low = matmul(down, x_ref[...], NT)
-    for b in range(N_X):
-        part[b] = low[:, b * BLOCK : (b + 1) * BLOCK].astype(jnp.bfloat16)
-    pl.semaphore_wait(barrier, N_TENSOR - 1)
-    wait_all(tensor_scatter(part, inbox, s1, r1))
-    tensor_reduce(inbox, full)
-    wait_all(tensor_gather(full, s2, r2))
-    low_ref[...] = full[...]
-
-
-def attention_kernel(
-    ids, base_ref, grad_ref, seg_ref, low_ref, up_ref, plow_ref, upout_ref,
-    kwin, vwin, ktrans, bias, qs, gs, dk_acc, dv_acc, gup_q, plow_q, up_half,
-):
-    i = pl.program_id(0)
-    adapter = ids[lax.axis_index("dp"), 0]
-    kcols = pl.ds(HEADS * HEAD, HEAD)
-    vcols = pl.ds((HEADS + 1) * HEAD, HEAD)
-    scale = 1.0 / math.sqrt(HEAD)
-
-    @pl.when(i == 0)
-    def _():
-        up_half[...] = (up_ref[adapter].astype(jnp.float32) * 0.5).astype(jnp.bfloat16)
-        kwin[BLOCK:] = jnp.zeros((BLOCK, HEAD), jnp.bfloat16)
-        vwin[BLOCK:] = jnp.zeros((BLOCK, HEAD), jnp.bfloat16)
-        dk_acc[...] = jnp.zeros_like(dk_acc)
-        dv_acc[...] = jnp.zeros_like(dv_acc)
-        gup_q[...] = jnp.zeros_like(gup_q)
-
-    low_q = low_ref[i, 0:RANK]
-    low_k = low_ref[i, RANK : 2 * RANK]
-    low_v = low_ref[i, 2 * RANK :]
-
-    kwin[:BLOCK] = kwin[BLOCK:]
-    vwin[:BLOCK] = vwin[BLOCK:]
-    key = base_ref[:, kcols].astype(jnp.float32) + matmul(low_k, up_half[:, kcols], TN)
-    value = base_ref[:, vcols].astype(jnp.float32) + matmul(low_v, up_half[:, vcols], TN)
-    kwin[BLOCK:] = key.astype(jnp.bfloat16)
-    vwin[BLOCK:] = value.astype(jnp.bfloat16)
-    ktrans[...] = kwin[...].astype(jnp.float32).T.astype(jnp.bfloat16)
-
-    now = seg_ref[0, pl.ds(pl.multiple_of(i * BLOCK, BLOCK), BLOCK)]
-    before = seg_ref[0, pl.ds(pl.multiple_of(jnp.maximum(i - 1, 0) * BLOCK, BLOCK), BLOCK)]
-    here = jnp.broadcast_to(now.astype(jnp.float32)[None, :], (BLOCK, BLOCK))
-    old = jnp.broadcast_to(before.astype(jnp.float32)[None, :], (BLOCK, BLOCK))
-    old = jnp.where(i == 0, -1.0, old)
-    u = lax.broadcasted_iota(jnp.int32, (BLOCK, BLOCK), 0)
-    t = lax.broadcasted_iota(jnp.int32, (BLOCK, BLOCK), 1)
-    bias[:BLOCK] = jnp.where(old.T == here, 0.0, masked_score)
-    bias[BLOCK:] = jnp.where((here.T == here) & (u <= t), 0.0, masked_score)
-
-    plow_q[...] = jnp.zeros_like(plow_q)
-    wide = STEP_HEADS * HEAD
-
-    def heads_step(s, carry):
-        cols = pl.ds(pl.multiple_of(s * wide, wide), wide)
-        up_here = up_half[:, cols]
-        q_wide = base_ref[:, cols].astype(jnp.float32) + matmul(low_q, up_here, TN)
-        q_wide = q_wide.astype(jnp.bfloat16)
-        g_wide = grad_ref[:, cols]
-        for h in range(STEP_HEADS):
-            qs[h * BLOCK : (h + 1) * BLOCK] = q_wide[:, h * HEAD : (h + 1) * HEAD]
-            gs[h * BLOCK : (h + 1) * BLOCK] = g_wide[:, h * HEAD : (h + 1) * HEAD]
-        q, g = qs[...], gs[...]
-        mask = jnp.concatenate([bias[...]] * STEP_HEADS, axis=1)
-        scores = matmul(kwin[...], q, NT) * (scale * math.log2(math.e)) + mask
-        top = jnp.max(scores, axis=0, keepdims=True)
-        weights = jnp.exp2(scores - top)
-        total = jnp.sum(weights, axis=0, keepdims=True)
-        probs = weights * (1.0 / total)
-        prob_grad = matmul(vwin[...], g, NT)
-        row_dot = jnp.sum(probs * prob_grad, axis=0, keepdims=True)
-        score_grad = (probs * (prob_grad - row_dot)).astype(jnp.bfloat16)
-        rows = pl.ds(pl.multiple_of(i * BLOCK, BLOCK), 2 * BLOCK)
-        dv_acc[rows] += matmul(probs.astype(jnp.bfloat16), g)
-        dk_acc[rows] += matmul(score_grad, q)
-        dq = (matmul(ktrans[...], score_grad) * scale).astype(jnp.bfloat16)
-        dq = jnp.concatenate(
-            [dq[:, h * BLOCK : (h + 1) * BLOCK] for h in range(STEP_HEADS)], axis=0
-        )
-        plow_q[...] += matmul(up_here, dq)
-        gup_q[:, cols] += matmul(low_q, dq, NT)
-        return carry
-
-    lax.fori_loop(0, HEADS // STEP_HEADS, heads_step, 0)
-    plow_ref[i, 0:RANK] = plow_q[...].astype(jnp.bfloat16)
-
-    @pl.when(i == pl.num_programs(0) - 1)
-    def _():
-        dk = (dk_acc[BLOCK:] * scale).astype(jnp.bfloat16)
-        dv = dv_acc[BLOCK:].astype(jnp.bfloat16)
-        part_k = matmul(up_half[:, kcols], dk, NT)
-        part_v = matmul(up_half[:, vcols], dv, NT)
-        gup_k = jnp.zeros((RANK, HEAD), jnp.float32)
-        gup_v = jnp.zeros((RANK, HEAD), jnp.float32)
-        for b in range(4):
-            own = slice(b * BLOCK, (b + 1) * BLOCK)
-            plow_ref[b, RANK : 2 * RANK] = part_k[:, own].astype(jnp.bfloat16)
-            plow_ref[b, 2 * RANK :] = part_v[:, own].astype(jnp.bfloat16)
-            gup_k += matmul(low_ref[b, RANK : 2 * RANK], dk[own])
-            gup_v += matmul(low_ref[b, 2 * RANK :], dv[own])
-        gup_k, gup_v = gup_k * 0.5, gup_v * 0.5
-        for j in range(CHIPS):
-            upout_ref[j, 0:RANK] = (gup_q[:, j * HEAD : (j + 1) * HEAD] * 0.5).astype(jnp.bfloat16)
-            mine = (adapter == j // 2).astype(jnp.float32)
-            upout_ref[j, RANK:] = ((gup_v if j % 2 else gup_k) * mine).astype(jnp.bfloat16)
+        copy.wait_recv()
+
+
+def sent(copies):
+    for copy in copies:
+        copy.wait_send()
 
 
 def split_dp():
@@ -279,7 +171,7 @@
 def sum_adapters(ids, inbox, rows, out, slot):
     def one(m, sums):
         term = inbox[m, rows].astype(jnp.float32)
-        adapter = ids[m, 0]
+        adapter = ids[m]
         return tuple(
             sums[a] + term * (adapter == a).astype(jnp.float32) for a in range(ADAPTERS)
         )
@@ -393,13 +285,122 @@
 STREAM_SEMS = [DMA((3,)), DMA((3,))] + [DMA((8,))] * 4 + [DMA((CHIPS,)), DMA]
 
 
-def adapters_kernel(
-    ids, x_ref, plow_ref, up_part, out_a, out_b, out_u,
-    inbox, full, s1, r1, s2, r2,
+def share(part, inbox, send, recv):
+    dp, me = lax.axis_index("dp"), lax.axis_index("tensor")
+    copies = []
+    for d in range(1, N_TENSOR):
+        copies.append(
+            pltpu.make_async_remote_copy(
+                src_ref=part,
+                dst_ref=inbox.at[me],
+                send_sem=send.at[d - 1],
+                recv_sem=recv.at[d - 1],
+                device_id=(dp, (me + d) % N_TENSOR),
+                device_id_type=MESH,
+            )
+        )
+        copies[-1].start()
+    inbox[me] = part[...]
+    return copies
+
+
+def attend(base, grad, seg, low, up_half, keys, values, qs, gs, plow, gup, upout, mine, done):
+    bf16, f32 = jnp.bfloat16, jnp.float32
+    qcols = slice(0, HEADS * HEAD)
+    kcols = slice(HEADS * HEAD, (HEADS + 1) * HEAD)
+    vcols = slice((HEADS + 1) * HEAD, (HEADS + 2) * HEAD)
+    scale = 1.0 / math.sqrt(HEAD)
+    for b in range(BLOCKS):
+        rows = slice(b * BLOCK, (b + 1) * BLOCK)
+        low_k, low_v = low[b, RANK : 2 * RANK], low[b, 2 * RANK :]
+        key = base[rows, kcols].astype(f32) + matmul(low_k, up_half[:, kcols], TN)
+        value = base[rows, vcols].astype(f32) + matmul(low_v, up_half[:, vcols], TN)
+        keys[rows] = key.astype(bf16)
+        values[rows] = value.astype(bf16)
+    u = lax.broadcasted_iota(jnp.int32, (BLOCK, BLOCK), 0)
+    t = lax.broadcasted_iota(jnp.int32, (BLOCK, BLOCK), 1)
+    docs = [
+        jnp.broadcast_to(
+            seg[:, b * BLOCK : (b + 1) * BLOCK].astype(f32), (BLOCK, BLOCK)
+        )
+        for b in range(BLOCKS)
+    ]
+    gup_k = jnp.zeros((RANK, HEAD), f32)
+    gup_v = jnp.zeros((RANK, HEAD), f32)
+    dk_next = dv_next = None
+    for i in reversed(range(BLOCKS)):
+        rows = slice(i * BLOCK, (i + 1) * BLOCK)
+        first = max(i - 1, 0)
+        window = slice(first * BLOCK, (i + 1) * BLOCK)
+        mask = jnp.where((docs[i].T == docs[i]) & (u <= t), 0.0, masked_score)
+        if first < i:
+            before = jnp.where(docs[first].T == docs[i], 0.0, masked_score)
+            mask = jnp.concatenate([before, mask], axis=0)
+        mask = jnp.concatenate([mask] * HEADS, axis=1)
+        key, value = keys[window], values[window]
+        low_q = low[i, 0:RANK]
+        up_q = up_half[:, qcols]
+        q_wide = (base[rows, qcols].astype(f32) + matmul(low_q, up_q, TN)).astype(bf16)
+        for h in range(HEADS):
+            qs[i % 2, h * BLOCK : (h + 1) * BLOCK] = q_wide[:, h * HEAD : (h + 1) * HEAD]
+        q, g = qs[i % 2], gs[i]
+        scores = matmul(key, q, NT) * (scale * math.log2(math.e)) + mask
+        top = jnp.max(scores, axis=0, keepdims=True)
+        weights = jnp.exp2(scores - top)
+        total = jnp.sum(weights, axis=0, keepdims=True)
+        probs = weights * (1.0 / total)
+        prob_grad = matmul(value, g, NT)
+        row_dot = jnp.sum(probs * prob_grad, axis=0, keepdims=True)
+        score_grad = (probs * (prob_grad - row_dot)).astype(bf16)
+        dv = matmul(probs.astype(bf16), g)
+        dk = matmul(score_grad, q)
+        dq = (matmul(key.astype(f32).T.astype(bf16), score_grad) * scale).astype(bf16)
+        dq = jnp.concatenate(
+            [dq[:, h * BLOCK : (h + 1) * BLOCK] for h in range(HEADS)], axis=0
+        )
+        part_q = matmul(up_q, dq)
+        if i == BLOCKS - 1:
+            gup[...] = matmul(low_q, dq, NT)
+            dk_own, dv_own = dk[BLOCK:], dv[BLOCK:]
+        else:
+            gup[...] += matmul(low_q, dq, NT)
+            dk_own, dv_own = dk[-BLOCK:] + dk_next, dv[-BLOCK:] + dv_next
+        dk_next, dv_next = dk[:BLOCK], dv[:BLOCK]
+        dk_own, dv_own = (dk_own * scale).astype(bf16), dv_own.astype(bf16)
+        plow[i, 0:RANK] = part_q.astype(bf16)
+        plow[i, RANK : 2 * RANK] = matmul(up_half[:, kcols], dk_own, NT).astype(bf16)
+        plow[i, 2 * RANK :] = matmul(up_half[:, vcols], dv_own, NT).astype(bf16)
+        done(i)
+        gup_k += matmul(low[i, RANK : 2 * RANK], dk_own)
+        gup_v += matmul(low[i, 2 * RANK :], dv_own)
+    gup_k, gup_v = gup_k * 0.5, gup_v * 0.5
+    for j in range(CHIPS):
+        upout[j, 0:RANK] = (gup[:, j * HEAD : (j + 1) * HEAD] * 0.5).astype(bf16)
+        upout[j, RANK:] = ((gup_v if j % 2 else gup_k) * mine(j // 2)).astype(bf16)
+
+
+def fused_kernel(
+    ids, x_hbm, base_hbm, grad_hbm, seg, down_hbm, up_hbm, out_a, out_b, out_u,
+    x_ref, base, grad, down_ref, up_ref, loads,
+    part, inbox, low, s1, r1, s2, r2,
+    up_half, keys, values, qs, gs, plow, gup, up_part, shared, s3, r3,
     down_a, down_b, in_a, in_b, in_u, sa, sb, su, ra, rb, ru, *sems,
 ):
+    bf16, f32 = jnp.bfloat16, jnp.float32
     chip, core = split_dp()
     tensor, dp = lax.axis_index("tensor"), lax.axis_index("dp")
+    fetch = [
+        pltpu.make_async_copy(src, dst, loads.at[n])
+        for n, (src, dst) in enumerate(
+            [
+                (down_hbm, down_ref), (x_hbm, x_ref), (up_hbm, up_ref),
+                (grad_hbm, grad), (base_hbm, base),
+            ]
+        )
+    ]
+    for copy in fetch:
+        copy.start()
+
     barrier = pltpu.get_barrier_semaphore()
     greet_tensor(barrier)
 
@@ -409,46 +410,61 @@
         return carry
 
     lax.fori_loop(1, MEMBERS, greet, 0)
+
+    adapter = ids[dp]
+    fetch[0].wait()
+    fetch[1].wait()
+    partial_low = matmul(down_ref[adapter], x_ref[...], NT)
+    for b in range(BLOCKS):
+        part[b] = partial_low[:, b * BLOCK : (b + 1) * BLOCK].astype(bf16)
     pl.semaphore_wait(barrier, N_TENSOR - 1 + MEMBERS - 1)
-
-    stream_a = Stream(out_a, 0, sems[0:8])
-    stream_b = Stream(out_b, 1, sems[8:16])
-    stream_u = Stream(out_u, 1, sems[16:24])
-
-    copies = tensor_scatter(plow_ref, inbox, s1, r1)
+    copies = tensor_scatter(part, inbox, s1, r1)
+    fetch[2].wait()
+    up_half[...] = (up_ref[adapter].astype(f32) * 0.5).astype(bf16)
+    fetch[3].wait()
+    for b in range(BLOCKS):
+        for h in range(HEADS):
+            tile = grad[b * BLOCK : (b + 1) * BLOCK, h * HEAD : (h + 1) * HEAD]
+            gs[b, h * BLOCK : (h + 1) * BLOCK] = tile
+    fetch[4].wait()
+    received(copies)
+    tensor_reduce(inbox, low)
+    more = tensor_gather(low, s2, r2)
+    received(more)
+    copies = copies + more
+
+    shares = []
+
+    def done(i):
+        shares.extend(share(plow.at[i], shared.at[i], s3.at[i], r3.at[i]))
+
+    def mine(a):
+        return (adapter == a).astype(f32)
+
+    attend(base, grad, seg, low, up_half, keys, values, qs, gs, plow, gup, up_part, mine, done)
     scatter(up_part, in_u, 1, su, ru)
-    wait_all(copies)
-    tensor_reduce(inbox, full)
-    copies = tensor_gather(full, s2, r2)
-
-    @pl.when(core == 1)
-    def _():
-        arrived(in_u, ru)
-        sum_adapters(ids, in_u, slice(0, RANK), out_u, chip)
-
-        def one(m, total):
-            return total + in_u[m, RANK:].astype(jnp.float32)
-
-        total = lax.fori_loop(0, MEMBERS, one, jnp.zeros((RANK, HEAD), jnp.float32))
-        out_u[chip, ADAPTERS] = total.astype(jnp.bfloat16)
-        stream_u.start()
-
-    wait_all(copies)
-    low_grad = jnp.concatenate([full[b] for b in range(N_X)], axis=1)
+
+    received(shares)
+    sums = []
+    for b in range(BLOCKS):
+        total = shared[b, 0].astype(f32)
+        for n in range(1, N_TENSOR):
+            total = total + shared[b, n].astype(f32)
+        sums.append(total.astype(bf16))
+    low_grad = jnp.concatenate(sums, axis=1)
     step = 4
-
-    def columns(s, carry):
-        cols = pl.ds(pl.multiple_of(s * (step * HEAD), step * HEAD), step * HEAD)
-        product = matmul(low_grad, x_ref[:, cols]).astype(jnp.bfloat16)
+    for s in range(CHIPS // step):
+        product = matmul(low_grad, x_ref[:, s * step * HEAD : (s + 1) * step * HEAD]).astype(bf16)
         for j in range(step):
             tile = product[:, j * HEAD : (j + 1) * HEAD]
             down_a[s * step + j] = tile[: 2 * RANK]
             down_b[s * step + j] = tile[2 * RANK :]
-        return carry
-
-    lax.fori_loop(0, CHIPS // step, columns, 0)
     scatter(down_a, in_a, 0, sa, ra)
     scatter(down_b, in_b, 1, sb, rb)
+
+    stream_a = Stream(out_a, 0, sems[0:8])
+    stream_b = Stream(out_b, 1, sems[8:16])
+    stream_u = Stream(out_u, 1, sems[16:24])
 
     @pl.when(core == 0)
     def _():
@@ -463,17 +479,27 @@
 
     @pl.when(core == 1)
     def _():
-        stream_u.spread()
+        arrived(in_u, ru)
+        sum_adapters(ids, in_u, slice(0, RANK), out_u, chip)
+
+        def one(m, total):
+            return total + in_u[m, RANK:].astype(f32)
+
+        total = lax.fori_loop(0, MEMBERS, one, jnp.zeros((RANK, HEAD), f32))
+        out_u[chip, ADAPTERS] = total.astype(bf16)
+        stream_u.start()
         arrived(in_b, rb)
         sum_adapters(ids, in_b, slice(0, RANK), out_b, chip)
         stream_b.start()
+        stream_u.spread()
+        stream_b.spread()
         stream_u.pass_on()
-        stream_b.spread()
         stream_b.pass_on()
         stream_u.finish()
         stream_b.finish()
         stream_a.receive()
 
+    sent(copies + shares)
     scatter_sent(up_part, in_u, 1, su, ru)
     scatter_sent(down_a, in_a, 0, sa, ra)
     scatter_sent(down_b, in_b, 1, sb, rb)
@@ -490,76 +516,42 @@
         up_ref[0, :, cols] = kv_ref[kind, 0].astype(jnp.float32)
 
 
+def hbm():
+    return pl.BlockSpec(memory_space=pl.ANY)
+
+
 def per_device(x, base, grad, segments, ids, down, up):
     bf16, f32 = jnp.bfloat16, jnp.float32
     tokens, width = x.shape
+    cols = base.shape[1]
     rows = KINDS * RANK
-    blocks = tokens // BLOCK
-    limit = 56 * 1024 * 1024
-
-    low = pl.pallas_call(
-        project_kernel,
-        out_shape=jax.ShapeDtypeStruct((blocks, rows, BLOCK), bf16),
-        in_specs=[smem(), vmem(), vmem()],
-        out_specs=vmem(),
-        scratch_shapes=[
-            VMEM((blocks, rows, BLOCK), bf16),
-            VMEM((N_TENSOR, rows, BLOCK), bf16),
-            VMEM((blocks, rows, BLOCK), bf16),
-            DMA((7,)), DMA((7,)), DMA((3,)), DMA((3,)),
-        ],
-        compiler_params=pltpu.CompilerParams(
-            collective_id=0, has_side_effects=True, vmem_limit_bytes=limit
-        ),
-        name="project",
-    )(ids, x, down)
-
-    cols = base.shape[1]
-    wide = STEP_HEADS * HEAD
-    plow, up_part = pl.pallas_call(
-        attention_kernel,
-        grid=(blocks,),
-        out_shape=(
-            jax.ShapeDtypeStruct((blocks, rows, BLOCK), bf16),
-            jax.ShapeDtypeStruct((CHIPS, 2 * RANK, HEAD), bf16),
-        ),
-        in_specs=[
-            smem(),
-            pl.BlockSpec((BLOCK, cols), lambda i: (i, 0)),
-            pl.BlockSpec((BLOCK, HEADS * HEAD), lambda i: (i, 0)),
-            vmem(), vmem(), vmem(),
-        ],
-        out_specs=(vmem(), vmem()),
-        scratch_shapes=[
-            VMEM((2 * BLOCK, HEAD), bf16),
-            VMEM((2 * BLOCK, HEAD), bf16),
-            VMEM((HEAD, 2 * BLOCK), bf16),
-            VMEM((2 * BLOCK, BLOCK), f32),
-            VMEM((wide, HEAD), bf16),
-            VMEM((wide, HEAD), bf16),
-            VMEM((tokens + BLOCK, HEAD), f32),
-            VMEM((tokens + BLOCK, HEAD), f32),
-            VMEM((RANK, HEADS * HEAD), f32),
-            VMEM((RANK, BLOCK), f32),
-            VMEM((RANK, cols), bf16),
-        ],
-        compiler_params=pltpu.CompilerParams(vmem_limit_bytes=limit),
-        name="attention",
-    )(ids, base, grad, segments, low, up)
-
+    limit = 58 * 1024 * 1024
     out_a, out_b, out_u = pl.pallas_call(
-        adapters_kernel,
+        fused_kernel,
         out_shape=(
             jax.ShapeDtypeStruct((CHIPS, ADAPTERS, 2 * RANK, HEAD), bf16),
             jax.ShapeDtypeStruct((CHIPS, ADAPTERS, RANK, HEAD), bf16),
             jax.ShapeDtypeStruct((CHIPS, ADAPTERS + 1, RANK, HEAD), bf16),
         ),
-        in_specs=[smem(), vmem(), vmem(), vmem()],
+        in_specs=[smem(), hbm(), hbm(), hbm(), vmem(), hbm(), hbm()],
         out_specs=(vmem(), vmem(), vmem()),
         scratch_shapes=[
+            VMEM(x.shape, bf16), VMEM(base.shape, bf16), VMEM(grad.shape, bf16),
+            VMEM(down.shape, bf16), VMEM(up.shape, bf16), DMA((5,)),
+            VMEM((BLOCKS, rows, BLOCK), bf16),
             VMEM((N_TENSOR, rows, BLOCK), bf16),
-            VMEM((blocks, rows, BLOCK), bf16),
+            VMEM((BLOCKS, rows, BLOCK), bf16),
             DMA((7,)), DMA((7,)), DMA((3,)), DMA((3,)),
+            VMEM((RANK, cols), bf16),
+            VMEM((tokens, HEAD), bf16),
+            VMEM((tokens, HEAD), bf16),
+            VMEM((2, HEADS * BLOCK, HEAD), bf16),
+            VMEM((BLOCKS, HEADS * BLOCK, HEAD), bf16),
+            VMEM((BLOCKS, rows, BLOCK), bf16),
+            VMEM((RANK, HEADS * HEAD), f32),
+            VMEM((CHIPS, 2 * RANK, HEAD), bf16),
+            VMEM((BLOCKS, N_TENSOR, rows, BLOCK), bf16),
+            DMA((BLOCKS, 7)), DMA((BLOCKS, 7)),
             VMEM((CHIPS, 2 * RANK, HEAD), bf16),
             VMEM((CHIPS, RANK, HEAD), bf16),
             VMEM((MEMBERS, 2 * RANK, HEAD), bf16),
@@ -569,10 +561,10 @@
             DMA, DMA, DMA,
         ] + STREAM_SEMS * 3,
         compiler_params=pltpu.CompilerParams(
-            collective_id=1, has_side_effects=True, vmem_limit_bytes=limit
+            collective_id=0, has_side_effects=True, vmem_limit_bytes=limit
         ),
-        name="adapters",
-    )(ids, x, plow, up_part)
+        name="fused",
+    )(ids.reshape(-1), x, base, grad, segments, down, up)
 
     return pl.pallas_call(
         widen_kernel,

time: 94.8 us -> 72.9 us (0.77)
  Pallas kernels: 92.5 us -> 72.1 us
  local copies, waits for them, and re-layouts: 1.33 us -> 0 us
    pallas_call x3 -> x1, Pallas kernels: 86.3 us -> 65.9 us  [per_device(): pl.pallas_call(fused_kernel, out_shape=(jax.ShapeDtypeStruct((CHIPS, ADAP...]
    unnamed x1 -> x0, local copies, waits for them, and re-layouts: 1.33 us -> none
where the time goes in v2:
time: 72.9 us; the launch traced here: 72.7 us
  Pallas kernels  72.1 us (99%)
    pallas_call x1, Pallas kernels, per_device(): pl.pallas_call(fused_kernel, out_shape=(jax.ShapeDtypeStruct((CHIPS, ADAP...  65.9 us
    pallas_call x1, Pallas kernels, per_device(): pl.pallas_call(widen_kernel, grid=(ADAPTERS,), out_shape=(jax.ShapeDtypeS...  6.16 us

profile of v2, /device:TPU:1, one launch (start us, length us, event | category | flops | bytes accessed | tf_op | source)
XLA Modules:
  0.0 72.7 jit_solution(17248533276903627299)
XLA Ops:
  0.6 65.9 %fused.1 = (bf16[16,8,32,128]{3,2,1,0:T(8,128)(2,1)}, bf16[16,8,16,128]{3,2,1,0:T(8,128)(2,1)}, bf16[16,9,16,128]{3,2,1,0:T(8,128)(2,1)}) custom-call(s32[32]{0:T(128)} %bitcast.1, bf16[512,2048]{1,0:T(8,128)(2,1)} %x_hbm.1, bf16[512,2304]{1,0:T(8,128)(2,1)} %base_hbm.1, bf16[512,2048]{1,0:T(8,128)(2,1)} %grad_hbm.1, s32[1,512]{1,0:T(1,128)} %seg.1, ...), custom_call_target="tpu_custom_call" | custom-call | tf_op jit(solution)/shard_map/fused/pallas_call | solution.py:529
  66.6 6.2 %widen.1 = (f32[8,48,2048]{2,1,0:T(8,128)}, f32[8,16,2304]{2,1,0:T(8,128)}) custom-call(bf16[16,8,32,128]{3,2,1,0:T(8,128)(2,1)} %get-tuple-element.5.a_ref, bf16[16,8,16,128]{3,2,1,0:T(8,128)(2,1)} %get-tuple-element.6.b_ref, bf16[16,9,16,128]{3,2,1,0:T(8,128)(2,1)} %get-tuple-element.7.u_ref.kv_ref, bf16[16,9,16,128]{3,2,1,0:T(8,128)(2,1)} %get-tuple-element.7.u_ref.kv_ref), custom_call_target="tpu_custom_call" | custom-call | tf_op jit(solution)/shard_map/widen/pallas_call | solution.py:569

commit v3 on v2

--- a/solution.py
+++ b/solution.py
@@ -26,6 +26,7 @@
 MEMBERS = 2 * CHIPS
 ADAPTERS = 8
 BLOCKS = 4
+STEP_ADAPTERS = 4
 masked_score = -1e30
 
 NT = (((1,), (1,)), ((), ()))
@@ -115,46 +116,46 @@
     return dp // 2, dp % 2
 
 
-def scatter(src, inbox, core_to, send, recv):
+def piece(src, inbox, p, core_to, send, recv):
     dp, tensor = lax.axis_index("dp"), lax.axis_index("tensor")
+    return pltpu.make_async_remote_copy(
+        src_ref=src.at[p],
+        dst_ref=inbox.at[dp],
+        send_sem=send,
+        recv_sem=recv,
+        device_id=(2 * p + core_to, tensor),
+        device_id_type=MESH,
+    )
+
+
+def own_piece(src, inbox, core_to, send, recv):
     chip, core = split_dp()
-
-    def one(k, carry):
-        p = (chip + k) % CHIPS
-        pltpu.make_async_remote_copy(
-            src_ref=src.at[p],
-            dst_ref=inbox.at[dp],
-            send_sem=send.at[k],
-            recv_sem=recv,
-            device_id=(2 * p + core_to, tensor),
-            device_id_type=MESH,
-        ).start()
-        return carry
-
-    lax.fori_loop(1, CHIPS, one, 0)
 
     @pl.when(core == core_to)
     def _():
-        pltpu.make_async_copy(src.at[chip], inbox.at[dp], recv).start()
+        pltpu.make_async_copy(src.at[chip], inbox.at[lax.axis_index("dp")], recv).start()
 
     @pl.when(core != core_to)
     def _():
-        one(0, 0)
+        piece(src, inbox, chip, core_to, send.at[0], recv).start()
+
+
+def scatter(src, inbox, core_to, send, recv):
+    chip, _ = split_dp()
+
+    def one(k, carry):
+        piece(src, inbox, (chip + k) % CHIPS, core_to, send.at[k], recv).start()
+        return carry
+
+    lax.fori_loop(1, CHIPS, one, 0)
+    own_piece(src, inbox, core_to, send, recv)
 
 
 def scatter_sent(src, inbox, core_to, send, recv):
-    dp, tensor = lax.axis_index("dp"), lax.axis_index("tensor")
     chip, core = split_dp()
 
     def one(k, carry):
-        pltpu.make_async_remote_copy(
-            src_ref=src.at[chip],
-            dst_ref=inbox.at[dp],
-            send_sem=send.at[k],
-            recv_sem=recv,
-            device_id=(2 * chip + core_to, tensor),
-            device_id_type=MESH,
-        ).wait_send()
+        piece(src, inbox, chip, core_to, send.at[k], recv).wait_send()
         return carry
 
     lax.fori_loop(1, CHIPS, one, 0)
@@ -183,106 +184,85 @@
 
 
 class Stream:
-    def __init__(self, out, owner, sems):
-        self.out, self.owner = out, owner
-        self.zs, self.zr, self.ys, self.yr, self.fs, self.fr, self.cs, self.cr = sems
-        self.half = out.shape[1] // 2
+    def __init__(self, buf, out, owner, sems):
+        self.buf, self.out, self.owner = buf, out, owner
+        self.zs, self.zr, self.ys, self.yr, self.cs, self.cr, self.ks = sems
         self.tensor = lax.axis_index("tensor")
         self.chip, self.core = split_dp()
         self.y, self.z = self.chip // N_Z, self.chip % N_Z
 
-    def copy(self, slot, chip_to, core_to, send, recv, part=None):
-        ref = self.out.at[slot] if part is None else self.out.at[slot, part]
+    def copy(self, slot, chip_to, core_to, send, recv, dst=None):
         return pltpu.make_async_remote_copy(
-            src_ref=ref,
-            dst_ref=ref,
+            src_ref=self.buf.at[slot],
+            dst_ref=(self.buf if dst is None else dst).at[slot],
             send_sem=send,
             recv_sem=recv,
             device_id=(2 * chip_to + core_to, self.tensor),
             device_id_type=MESH,
         )
 
-    def at(self, y, z):
-        return (y % N_Y) * N_Z + z % N_Z
+    def at(self, dy, dz):
+        return ((self.y + dy + N_Y) % N_Y) * N_Z + (self.z + dz + N_Z) % N_Z
+
+    def nearest_first(self):
+        z, high = self.z, self.z // 2
+        sources = (z + 1 - 2 * (z % 2), 2 - high, 3 * (1 - high))
+        return [(z - source + N_Z) % N_Z for source in sources]
 
     def z_copy(self, d):
         return self.copy(
-            self.chip, self.at(self.y, self.z + d), self.owner, self.zs.at[d - 1], self.zr.at[d - 1]
-        )
-
-    def y_copy(self, dz, side):
-        to = self.at(self.y + (1 if side == 0 else 3), self.z)
-        slot = self.at(self.y, self.z + N_Z - dz)
-        n = 2 * dz + side
-        return self.copy(slot, to, self.owner, self.ys.at[n], self.yr.at[n])
-
-    def y_arrival(self, dz, side):
-        n = 2 * dz + side
+            self.chip, self.at(0, d), self.owner, self.zs.at[d - 1], self.zr.at[d - 1]
+        )
+
+    def y_copy(self, dz, dy):
+        n = 3 * dz + dy - 1
+        return self.copy(self.at(0, -dz), self.at(dy, 0), self.owner, self.ys.at[n], self.yr.at[n])
+
+    def twin(self, n, slot):
         return self.copy(
-            self.y_slot(dz, side), self.chip, self.owner, self.ys.at[n], self.yr.at[n]
-        )
-
-    def y_slot(self, dz, side):
-        return self.at(self.y + (3 if side == 0 else 1), self.z + N_Z - dz)
-
-    def part(self, side):
-        n = self.out.shape[1]
-        return pl.ds(0, self.half) if side == 0 else pl.ds(self.half, n - self.half)
-
-    def forward(self, dz, side):
-        to = self.at(self.y + (1 if side == 0 else 3), self.z)
-        slot = self.y_slot(dz, side)
-        n = 2 * dz + side
-        return self.copy(slot, to, self.owner, self.fs.at[n], self.fr.at[n], self.part(side))
-
-    def forwarded(self, dz, side):
-        slot = self.at(self.y + 2, self.z + N_Z - dz)
-        n = 2 * dz + side
-        return self.copy(slot, self.chip, self.owner, self.fs.at[n], self.fr.at[n], self.part(side))
-
-    def twin(self, n, slot):
-        return self.copy(slot, self.chip, 1 - self.owner, self.cs.at[n], self.cr)
+            slot, self.chip, 1 - self.owner, self.cs.at[n], self.cr, self.out
+        )
+
+    def deliver(self, n, slot):
+        self.twin(n, slot).start()
+        pltpu.make_async_copy(self.buf.at[slot], self.out.at[slot], self.ks).start()
+
+    def y_sends(self, dz):
+        for dy in (2, 1, 3):
+            self.y_copy(dz, dy).start()
+        self.deliver(dz, self.at(0, -dz))
 
     def start(self):
-        for d in (1, 3, 2):
+        for d in (2, 1, 3):
             self.z_copy(d).start()
-        for side in range(2):
-            self.y_copy(0, side).start()
-        self.twin(0, self.chip).start()
+        self.y_sends(0)
 
     def spread(self):
-        for dz in (1, 3, 2):
+        for dz in self.nearest_first():
             self.z_copy(dz).wait_recv()
-            for side in range(2):
-                self.y_copy(dz, side).start()
-            self.twin(dz, self.at(self.y, self.z + N_Z - dz)).start()
-
-    def pass_on(self):
-        for dz in (0, 1, 3, 2):
-            for side in range(2):
-                self.y_arrival(dz, side).wait_recv()
-                self.forward(dz, side).start()
-                self.twin(4 + 2 * dz + side, self.y_slot(dz, side)).start()
+            self.y_sends(dz)
 
     def finish(self):
-        for dz in (0, 1, 3, 2):
-            for side in range(2):
-                self.forwarded(dz, side).wait_recv()
-            self.twin(12 + dz, self.at(self.y + 2, self.z + N_Z - dz)).start()
+        for dz in [0] + self.nearest_first():
+            for dy in (1, 3, 2):
+                self.y_copy(dz, dy).wait_recv()
+                self.deliver(4 + 3 * dz + dy - 1, self.at(-dy, -dz))
+
+    def sent(self):
         for d in range(1, N_Z):
             self.z_copy(d).wait_send()
         for dz in range(N_Z):
-            for side in range(2):
-                self.y_copy(dz, side).wait_send()
-                self.forward(dz, side).wait_send()
+            for dy in range(1, N_Y):
+                self.y_copy(dz, dy).wait_send()
         for n in range(CHIPS):
             self.twin(n, self.chip).wait_send()
+        pltpu.make_async_copy(self.buf, self.out, self.ks).wait()
 
     def receive(self):
         arrived(self.out, self.cr)
 
 
-STREAM_SEMS = [DMA((3,)), DMA((3,))] + [DMA((8,))] * 4 + [DMA((CHIPS,)), DMA]
+STREAM_SEMS = [DMA((3,)), DMA((3,)), DMA((12,)), DMA((12,)), DMA((CHIPS,)), DMA, DMA]
 
 
 def share(part, inbox, send, recv):
@@ -384,7 +364,8 @@
     x_ref, base, grad, down_ref, up_ref, loads,
     part, inbox, low, s1, r1, s2, r2,
     up_half, keys, values, qs, gs, plow, gup, up_part, shared, s3, r3,
-    down_a, down_b, in_a, in_b, in_u, sa, sb, su, ra, rb, ru, *sems,
+    down_early, down_a, down_b, in_a, in_b, in_u, sa, sb, su, ra, rb, ru,
+    buf_a, buf_b, buf_u, *sems,
 ):
     bf16, f32 = jnp.bfloat16, jnp.float32
     chip, core = split_dp()
@@ -433,10 +414,10 @@
     received(more)
     copies = copies + more
 
-    shares = []
+    shares = {}
 
     def done(i):
-        shares.extend(share(plow.at[i], shared.at[i], s3.at[i], r3.at[i]))
+        shares[i] = share(plow.at[i], shared.at[i], s3.at[i], r3.at[i])
 
     def mine(a):
         return (adapter == a).astype(f32)
@@ -444,62 +425,78 @@
     attend(base, grad, seg, low, up_half, keys, values, qs, gs, plow, gup, up_part, mine, done)
     scatter(up_part, in_u, 1, su, ru)
 
-    received(shares)
-    sums = []
-    for b in range(BLOCKS):
+    def low_grad(b):
+        received(shares[b])
         total = shared[b, 0].astype(f32)
         for n in range(1, N_TENSOR):
             total = total + shared[b, n].astype(f32)
-        sums.append(total.astype(bf16))
-    low_grad = jnp.concatenate(sums, axis=1)
-    step = 4
-    for s in range(CHIPS // step):
-        product = matmul(low_grad, x_ref[:, s * step * HEAD : (s + 1) * step * HEAD]).astype(bf16)
-        for j in range(step):
+        return total.astype(bf16)
+
+    early = jnp.concatenate([low_grad(b) for b in range(1, BLOCKS)], axis=1)
+    wide = N_Z * HEAD
+    for s in range(N_Y):
+        cols = slice(s * wide, (s + 1) * wide)
+        down_early[:, cols] = matmul(early, x_ref[BLOCK:, cols])
+    late = low_grad(0)
+    y, z = chip // N_Z, chip % N_Z
+    for s, dy in enumerate((2, 1, 3, 0)):
+        there = (y + dy) % N_Y
+        cols = pl.ds(pl.multiple_of(there * wide, wide), wide)
+        product = (matmul(late, x_ref[:BLOCK, cols]) + down_early[:, cols]).astype(bf16)
+        for j in range(N_Z):
             tile = product[:, j * HEAD : (j + 1) * HEAD]
-            down_a[s * step + j] = tile[: 2 * RANK]
-            down_b[s * step + j] = tile[2 * RANK :]
-    scatter(down_a, in_a, 0, sa, ra)
-    scatter(down_b, in_b, 1, sb, rb)
-
-    stream_a = Stream(out_a, 0, sems[0:8])
-    stream_b = Stream(out_b, 1, sems[8:16])
-    stream_u = Stream(out_u, 1, sems[16:24])
+            down_a[there * N_Z + j] = tile[: 2 * RANK]
+            down_b[there * N_Z + j] = tile[2 * RANK :]
+        for j in range(N_Z):
+            if dy:
+                p = there * N_Z + (1 - z // 2) * (3 - j) + (z // 2) * j
+            else:
+                p = there * N_Z + (z + j) % N_Z
+            n = (4 + 4 * s + j) if dy else j
+            if dy or j:
+                piece(down_a, in_a, p, 0, sa.at[n], ra).start()
+                piece(down_b, in_b, p, 1, sb.at[n], rb).start()
+    own_piece(down_a, in_a, 0, sa, ra)
+    own_piece(down_b, in_b, 1, sb, rb)
+
+    stream_a = Stream(buf_a, out_a, 0, sems[0:7])
+    stream_b = Stream(buf_b, out_b, 1, sems[7:14])
+    stream_u = Stream(buf_u, out_u, 1, sems[14:21])
 
     @pl.when(core == 0)
     def _():
         arrived(in_a, ra)
-        sum_adapters(ids, in_a, slice(0, 2 * RANK), out_a, chip)
+        sum_adapters(ids, in_a, slice(0, 2 * RANK), buf_a, chip)
         stream_a.start()
         stream_a.spread()
-        stream_a.pass_on()
         stream_a.finish()
+        stream_a.sent()
         stream_b.receive()
         stream_u.receive()
 
     @pl.when(core == 1)
     def _():
         arrived(in_u, ru)
-        sum_adapters(ids, in_u, slice(0, RANK), out_u, chip)
+        sum_adapters(ids, in_u, slice(0, RANK), buf_u, chip)
 
         def one(m, total):
             return total + in_u[m, RANK:].astype(f32)
 
         total = lax.fori_loop(0, MEMBERS, one, jnp.zeros((RANK, HEAD), f32))
-        out_u[chip, ADAPTERS] = total.astype(bf16)
+        buf_u[chip, ADAPTERS] = total.astype(bf16)
         stream_u.start()
         arrived(in_b, rb)
-        sum_adapters(ids, in_b, slice(0, RANK), out_b, chip)
+        sum_adapters(ids, in_b, slice(0, RANK), buf_b, chip)
         stream_b.start()
         stream_u.spread()
         stream_b.spread()
-        stream_u.pass_on()
-        stream_b.pass_on()
         stream_u.finish()
         stream_b.finish()
+        stream_u.sent()
+        stream_b.sent()
         stream_a.receive()
 
-    sent(copies + shares)
+    sent(copies + sum(shares.values(), []))
     scatter_sent(up_part, in_u, 1, su, ru)
     scatter_sent(down_a, in_a, 0, sa, ra)
     scatter_sent(down_b, in_b, 1, sb, rb)
@@ -508,12 +505,13 @@
 def widen_kernel(a_ref, b_ref, u_ref, kv_ref, down_ref, up_ref):
     for j in range(CHIPS):
         cols = slice(j * HEAD, (j + 1) * HEAD)
-        down_ref[0, : 2 * RANK, cols] = a_ref[j, 0].astype(jnp.float32)
-        down_ref[0, 2 * RANK :, cols] = b_ref[j, 0].astype(jnp.float32)
-        up_ref[0, :, cols] = u_ref[j, 0].astype(jnp.float32)
+        down_ref[:, : 2 * RANK, cols] = a_ref[j].astype(jnp.float32)
+        down_ref[:, 2 * RANK :, cols] = b_ref[j].astype(jnp.float32)
+        up_ref[:, :, cols] = u_ref[j].astype(jnp.float32)
     for kind in range(2):
         cols = slice((CHIPS + kind) * HEAD, (CHIPS + kind + 1) * HEAD)
-        up_ref[0, :, cols] = kv_ref[kind, 0].astype(jnp.float32)
+        for a in range(STEP_ADAPTERS):
+            up_ref[a, :, cols] = kv_ref[2 * a + kind, 0].astype(jnp.float32)
 
 
 def hbm():
@@ -534,7 +532,7 @@
             jax.ShapeDtypeStruct((CHIPS, ADAPTERS + 1, RANK, HEAD), bf16),
         ),
         in_specs=[smem(), hbm(), hbm(), hbm(), vmem(), hbm(), hbm()],
-        out_specs=(vmem(), vmem(), vmem()),
+        out_specs=(hbm(), hbm(), hbm()),
         scratch_shapes=[
             VMEM(x.shape, bf16), VMEM(base.shape, bf16), VMEM(grad.shape, bf16),
             VMEM(down.shape, bf16), VMEM(up.shape, bf16), DMA((5,)),
@@ -552,6 +550,7 @@
             VMEM((CHIPS, 2 * RANK, HEAD), bf16),
             VMEM((BLOCKS, N_TENSOR, rows, BLOCK), bf16),
             DMA((BLOCKS, 7)), DMA((BLOCKS, 7)),
+            VMEM((rows, width), f32),
             VMEM((CHIPS, 2 * RANK, HEAD), bf16),
             VMEM((CHIPS, RANK, HEAD), bf16),
             VMEM((MEMBERS, 2 * RANK, HEAD), bf16),
@@ -559,6 +558,9 @@
             VMEM((MEMBERS, 2 * RANK, HEAD), bf16),
             DMA((CHIPS,)), DMA((CHIPS,)), DMA((CHIPS,)),
             DMA, DMA, DMA,
+            VMEM((CHIPS, ADAPTERS, 2 * RANK, HEAD), bf16),
+            VMEM((CHIPS, ADAPTERS, RANK, HEAD), bf16),
+            VMEM((CHIPS, ADAPTERS + 1, RANK, HEAD), bf16),
         ] + STREAM_SEMS * 3,
         compiler_params=pltpu.CompilerParams(
             collective_id=0, has_side_effects=True, vmem_limit_bytes=limit
@@ -568,20 +570,20 @@
 
     return pl.pallas_call(
         widen_kernel,
-        grid=(ADAPTERS,),
+        grid=(ADAPTERS // STEP_ADAPTERS,),
         out_shape=(
             jax.ShapeDtypeStruct((ADAPTERS, rows, width), f32),
             jax.ShapeDtypeStruct((ADAPTERS, RANK, cols), f32),
         ),
         in_specs=[
-            pl.BlockSpec((CHIPS, 1, 2 * RANK, HEAD), lambda a: (0, a, 0, 0)),
-            pl.BlockSpec((CHIPS, 1, RANK, HEAD), lambda a: (0, a, 0, 0)),
-            pl.BlockSpec((CHIPS, 1, RANK, HEAD), lambda a: (0, a, 0, 0)),
-            pl.BlockSpec((2, 1, RANK, HEAD), lambda a: (a, ADAPTERS, 0, 0)),
+            pl.BlockSpec((CHIPS, STEP_ADAPTERS, 2 * RANK, HEAD), lambda a: (0, a, 0, 0)),
+            pl.BlockSpec((CHIPS, STEP_ADAPTERS, RANK, HEAD), lambda a: (0, a, 0, 0)),
+            pl.BlockSpec((CHIPS, STEP_ADAPTERS, RANK, HEAD), lambda a: (0, a, 0, 0)),
+            pl.BlockSpec((2 * STEP_ADAPTERS, 1, RANK, HEAD), lambda a: (a, ADAPTERS, 0, 0)),
         ],
         out_specs=(
-            pl.BlockSpec((1, rows, width), lambda a: (a, 0, 0)),
-            pl.BlockSpec((1, RANK, cols), lambda a: (a, 0, 0)),
+            pl.BlockSpec((STEP_ADAPTERS, rows, width), lambda a: (a, 0, 0)),
+            pl.BlockSpec((STEP_ADAPTERS, RANK, cols), lambda a: (a, 0, 0)),
         ),
         compiler_params=pltpu.CompilerParams(vmem_limit_bytes=limit),
         name="widen",

time: 72.9 us -> 66.5 us (0.912)
  Pallas kernels: 72.1 us -> 65.7 us
    pallas_call x1, Pallas kernels: 65.9 us -> 62.2 us  [per_device(): pl.pallas_call(fused_kernel, out_shape=(jax.ShapeDtypeStruct((CHIPS, ADAP...]
    pallas_call x1, Pallas kernels: 6.16 us -> 3.48 us  [per_device(): pl.pallas_call(widen_kernel, grid=(ADAPTERS // STEP_ADAPTERS,), out_shape...]
where the time goes in v3:
time: 66.5 us; the launch traced here: 66.3 us
  Pallas kernels  65.7 us (99%)
    pallas_call x1, Pallas kernels, per_device(): pl.pallas_call(fused_kernel, out_shape=(jax.ShapeDtypeStruct((CHIPS, ADAP...  62.2 us
    pallas_call x1, Pallas kernels, per_device(): pl.pallas_call(widen_kernel, grid=(ADAPTERS // STEP_ADAPTERS,), out_shape...  3.48 us

profile of v3, /device:TPU:1, one launch (start us, length us, event | category | flops | bytes accessed | tf_op | source)
XLA Modules:
  0.0 66.3 jit_solution(11687091778915802431)
XLA Ops:
  0.6 62.2 %fused.1 = (bf16[16,8,32,128]{3,2,1,0:T(8,128)(2,1)}, bf16[16,8,16,128]{3,2,1,0:T(8,128)(2,1)}, bf16[16,9,16,128]{3,2,1,0:T(8,128)(2,1)}) custom-call(s32[32]{0:T(128)} %bitcast.1, bf16[512,2048]{1,0:T(8,128)(2,1)} %x_hbm.1, bf16[512,2304]{1,0:T(8,128)(2,1)} %base_hbm.1, bf16[512,2048]{1,0:T(8,128)(2,1)} %grad_hbm.1, s32[1,512]{1,0:T(1,128)} %seg.1, ...), custom_call_target="tpu_custom_call" | custom-call | tf_op jit(solution)/shard_map/fused/pallas_call | solution.py:527
  62.8 3.5 %widen.1 = (f32[8,48,2048]{2,1,0:T(8,128)}, f32[8,16,2304]{2,1,0:T(8,128)}) custom-call(bf16[16,8,32,128]{3,2,1,0:T(8,128)(2,1)} %get-tuple-element.5.a_ref, bf16[16,8,16,128]{3,2,1,0:T(8,128)(2,1)} %get-tuple-element.6.b_ref, bf16[16,9,16,128]{3,2,1,0:T(8,128)(2,1)} %get-tuple-element.7.u_ref.kv_ref, bf16[16,9,16,128]{3,2,1,0:T(8,128)(2,1)} %get-tuple-element.7.u_ref.kv_ref), custom_call_target="tpu_custom_call" | custom-call | tf_op jit(solution)/shard_map/widen/pallas_call | solution.py:571

commit v4 on v3

--- a/solution.py
+++ b/solution.py
@@ -26,7 +26,6 @@
 MEMBERS = 2 * CHIPS
 ADAPTERS = 8
 BLOCKS = 4
-STEP_ADAPTERS = 4
 masked_score = -1e30
 
 NT = (((1,), (1,)), ((), ()))
@@ -284,86 +283,102 @@
     return copies
 
 
-def attend(base, grad, seg, low, up_half, keys, values, qs, gs, plow, gup, upout, mine, done):
+def fill_masks(seg, masks):
+    u = lax.broadcasted_iota(jnp.int32, (BLOCK, BLOCK), 0)
+    t = lax.broadcasted_iota(jnp.int32, (BLOCK, BLOCK), 1)
+    docs = [
+        jnp.broadcast_to(
+            seg[:, b * BLOCK : (b + 1) * BLOCK].astype(jnp.float32), (BLOCK, BLOCK)
+        )
+        for b in range(BLOCKS)
+    ]
+    for i in range(BLOCKS):
+        masks[i, BLOCK:] = jnp.where((docs[i].T == docs[i]) & (u <= t), 0.0, masked_score)
+        if i:
+            masks[i, :BLOCK] = jnp.where(docs[i - 1].T == docs[i], 0.0, masked_score)
+
+
+ORDER = "A3 B3 A2 C3 B2 A1 C2 B1 A0 C1 B0 C0".split()
+
+
+def attend(base, masks, low, up_half, keys, values, gs, dqs, plow, upout, mine, done):
     bf16, f32 = jnp.bfloat16, jnp.float32
     qcols = slice(0, HEADS * HEAD)
     kcols = slice(HEADS * HEAD, (HEADS + 1) * HEAD)
     vcols = slice((HEADS + 1) * HEAD, (HEADS + 2) * HEAD)
     scale = 1.0 / math.sqrt(HEAD)
-    for b in range(BLOCKS):
-        rows = slice(b * BLOCK, (b + 1) * BLOCK)
-        low_k, low_v = low[b, RANK : 2 * RANK], low[b, 2 * RANK :]
-        key = base[rows, kcols].astype(f32) + matmul(low_k, up_half[:, kcols], TN)
-        value = base[rows, vcols].astype(f32) + matmul(low_v, up_half[:, vcols], TN)
-        keys[rows] = key.astype(bf16)
-        values[rows] = value.astype(bf16)
-    u = lax.broadcasted_iota(jnp.int32, (BLOCK, BLOCK), 0)
-    t = lax.broadcasted_iota(jnp.int32, (BLOCK, BLOCK), 1)
-    docs = [
-        jnp.broadcast_to(
-            seg[:, b * BLOCK : (b + 1) * BLOCK].astype(f32), (BLOCK, BLOCK)
-        )
-        for b in range(BLOCKS)
-    ]
-    gup_k = jnp.zeros((RANK, HEAD), f32)
-    gup_v = jnp.zeros((RANK, HEAD), f32)
-    dk_next = dv_next = None
-    for i in reversed(range(BLOCKS)):
+    low_q, low_k, low_v = (
+        jnp.concatenate([low[b, n * RANK : (n + 1) * RANK] for b in range(BLOCKS)], axis=1)
+        for n in range(KINDS)
+    )
+    keys[...] = (base[:, kcols].astype(f32) + matmul(low_k, up_half[:, kcols], TN)).astype(bf16)
+    values[...] = (base[:, vcols].astype(f32) + matmul(low_v, up_half[:, vcols], TN)).astype(bf16)
+    up_q = up_half[:, qcols]
+    held, grads, next_dk, next_dv = {}, {}, {}, {}
+    own_k, own_v = {}, {}
+
+    def window(i):
+        return slice(max(i - 1, 0) * BLOCK, (i + 1) * BLOCK)
+
+    def stage_a(i):
         rows = slice(i * BLOCK, (i + 1) * BLOCK)
-        first = max(i - 1, 0)
-        window = slice(first * BLOCK, (i + 1) * BLOCK)
-        mask = jnp.where((docs[i].T == docs[i]) & (u <= t), 0.0, masked_score)
-        if first < i:
-            before = jnp.where(docs[first].T == docs[i], 0.0, masked_score)
-            mask = jnp.concatenate([before, mask], axis=0)
+        q_wide = base[rows, qcols].astype(f32) + matmul(low[i, 0:RANK], up_q, TN)
+        q_wide = q_wide.astype(bf16)
+        q = jnp.concatenate([q_wide[:, h * HEAD : (h + 1) * HEAD] for h in range(HEADS)], axis=0)
+        held[i] = q, matmul(keys[window(i)], q, NT)
+
+    def stage_b(i):
+        q, scores = held.pop(i)
+        mask = masks[i] if i else masks[0, BLOCK:]
         mask = jnp.concatenate([mask] * HEADS, axis=1)
-        key, value = keys[window], values[window]
-        low_q = low[i, 0:RANK]
-        up_q = up_half[:, qcols]
-        q_wide = (base[rows, qcols].astype(f32) + matmul(low_q, up_q, TN)).astype(bf16)
-        for h in range(HEADS):
-            qs[i % 2, h * BLOCK : (h + 1) * BLOCK] = q_wide[:, h * HEAD : (h + 1) * HEAD]
-        q, g = qs[i % 2], gs[i]
-        scores = matmul(key, q, NT) * (scale * math.log2(math.e)) + mask
+        scores = scores * (scale * math.log2(math.e)) + mask
         top = jnp.max(scores, axis=0, keepdims=True)
         weights = jnp.exp2(scores - top)
         total = jnp.sum(weights, axis=0, keepdims=True)
         probs = weights * (1.0 / total)
-        prob_grad = matmul(value, g, NT)
+        prob_grad = matmul(values[window(i)], gs[i], NT)
         row_dot = jnp.sum(probs * prob_grad, axis=0, keepdims=True)
         score_grad = (probs * (prob_grad - row_dot)).astype(bf16)
-        dv = matmul(probs.astype(bf16), g)
+        grads[i] = q, probs.astype(bf16), score_grad
+
+    def stage_c(i):
+        q, probs, score_grad = grads.pop(i)
         dk = matmul(score_grad, q)
+        dv = matmul(probs, gs[i])
+        key = keys[window(i)]
         dq = (matmul(key.astype(f32).T.astype(bf16), score_grad) * scale).astype(bf16)
         dq = jnp.concatenate(
             [dq[:, h * BLOCK : (h + 1) * BLOCK] for h in range(HEADS)], axis=0
         )
-        part_q = matmul(up_q, dq)
-        if i == BLOCKS - 1:
-            gup[...] = matmul(low_q, dq, NT)
-            dk_own, dv_own = dk[BLOCK:], dv[BLOCK:]
-        else:
-            gup[...] += matmul(low_q, dq, NT)
-            dk_own, dv_own = dk[-BLOCK:] + dk_next, dv[-BLOCK:] + dv_next
-        dk_next, dv_next = dk[:BLOCK], dv[:BLOCK]
-        dk_own, dv_own = (dk_own * scale).astype(bf16), dv_own.astype(bf16)
-        plow[i, 0:RANK] = part_q.astype(bf16)
-        plow[i, RANK : 2 * RANK] = matmul(up_half[:, kcols], dk_own, NT).astype(bf16)
-        plow[i, 2 * RANK :] = matmul(up_half[:, vcols], dv_own, NT).astype(bf16)
+        dqs[:, i * BLOCK : (i + 1) * BLOCK] = dq
+        dk_own, dv_own = dk[-BLOCK:], dv[-BLOCK:]
+        if i < BLOCKS - 1:
+            dk_own, dv_own = dk_own + next_dk.pop(i), dv_own + next_dv.pop(i)
+        if i:
+            next_dk[i - 1], next_dv[i - 1] = dk[:BLOCK], dv[:BLOCK]
+        own_k[i], own_v[i] = (dk_own * scale).astype(bf16), dv_own.astype(bf16)
+        plow[i, 0:RANK] = matmul(up_q, dq).astype(bf16)
+        plow[i, RANK : 2 * RANK] = matmul(up_half[:, kcols], own_k[i], NT).astype(bf16)
+        plow[i, 2 * RANK :] = matmul(up_half[:, vcols], own_v[i], NT).astype(bf16)
         done(i)
-        gup_k += matmul(low[i, RANK : 2 * RANK], dk_own)
-        gup_v += matmul(low[i, 2 * RANK :], dv_own)
-    gup_k, gup_v = gup_k * 0.5, gup_v * 0.5
+
+    stages = {"A": stage_a, "B": stage_b, "C": stage_c}
+    for item in ORDER:
+        stages[item[0]](int(item[1]))
+
+    gup = matmul(low_q, dqs[...], NT) * 0.5
+    gup_k = sum(matmul(low[b, RANK : 2 * RANK], own_k[b]) for b in range(BLOCKS)) * 0.5
+    gup_v = sum(matmul(low[b, 2 * RANK :], own_v[b]) for b in range(BLOCKS)) * 0.5
     for j in range(CHIPS):
-        upout[j, 0:RANK] = (gup[:, j * HEAD : (j + 1) * HEAD] * 0.5).astype(bf16)
+        upout[j, 0:RANK] = gup[:, j * HEAD : (j + 1) * HEAD].astype(bf16)
         upout[j, RANK:] = ((gup_v if j % 2 else gup_k) * mine(j // 2)).astype(bf16)
 
 
 def fused_kernel(
-    ids, x_hbm, base_hbm, grad_hbm, seg, down_hbm, up_hbm, out_a, out_b, out_u,
-    x_ref, base, grad, down_ref, up_ref, loads,
+    ids_hbm, x_hbm, base_hbm, grad_hbm, seg_hbm, down_hbm, up_hbm, out_a, out_b, out_u,
+    ids, x_ref, base, grad, seg, down_ref, up_ref, masks, loads,
     part, inbox, low, s1, r1, s2, r2,
-    up_half, keys, values, qs, gs, plow, gup, up_part, shared, s3, r3,
+    up_half, keys, values, gs, dqs, plow, up_part, shared, s3, r3,
     down_early, down_a, down_b, in_a, in_b, in_u, sa, sb, su, ra, rb, ru,
     buf_a, buf_b, buf_u, *sems,
 ):
@@ -374,8 +389,8 @@
         pltpu.make_async_copy(src, dst, loads.at[n])
         for n, (src, dst) in enumerate(
             [
-                (down_hbm, down_ref), (x_hbm, x_ref), (up_hbm, up_ref),
-                (grad_hbm, grad), (base_hbm, base),
+                (ids_hbm, ids), (down_hbm, down_ref), (x_hbm, x_ref), (up_hbm, up_ref),
+                (grad_hbm, grad), (base_hbm, base), (seg_hbm, seg),
             ]
         )
     ]
@@ -392,22 +407,25 @@
 
     lax.fori_loop(1, MEMBERS, greet, 0)
 
+    fetch[0].wait()
     adapter = ids[dp]
-    fetch[0].wait()
     fetch[1].wait()
+    fetch[2].wait()
     partial_low = matmul(down_ref[adapter], x_ref[...], NT)
     for b in range(BLOCKS):
         part[b] = partial_low[:, b * BLOCK : (b + 1) * BLOCK].astype(bf16)
     pl.semaphore_wait(barrier, N_TENSOR - 1 + MEMBERS - 1)
     copies = tensor_scatter(part, inbox, s1, r1)
-    fetch[2].wait()
+    fetch[3].wait()
     up_half[...] = (up_ref[adapter].astype(f32) * 0.5).astype(bf16)
-    fetch[3].wait()
+    fetch[6].wait()
+    fill_masks(seg, masks)
+    fetch[4].wait()
     for b in range(BLOCKS):
         for h in range(HEADS):
             tile = grad[b * BLOCK : (b + 1) * BLOCK, h * HEAD : (h + 1) * HEAD]
             gs[b, h * BLOCK : (h + 1) * BLOCK] = tile
-    fetch[4].wait()
+    fetch[5].wait()
     received(copies)
     tensor_reduce(inbox, low)
     more = tensor_gather(low, s2, r2)
@@ -422,7 +440,7 @@
     def mine(a):
         return (adapter == a).astype(f32)
 
-    attend(base, grad, seg, low, up_half, keys, values, qs, gs, plow, gup, up_part, mine, done)
+    attend(base, masks, low, up_half, keys, values, gs, dqs, plow, up_part, mine, done)
     scatter(up_part, in_u, 1, su, ru)
 
     def low_grad(b):
@@ -502,16 +520,38 @@
     scatter_sent(down_b, in_b, 1, sb, rb)
 
 
-def widen_kernel(a_ref, b_ref, u_ref, kv_ref, down_ref, up_ref):
-    for j in range(CHIPS):
-        cols = slice(j * HEAD, (j + 1) * HEAD)
-        down_ref[:, : 2 * RANK, cols] = a_ref[j].astype(jnp.float32)
-        down_ref[:, 2 * RANK :, cols] = b_ref[j].astype(jnp.float32)
-        up_ref[:, :, cols] = u_ref[j].astype(jnp.float32)
-    for kind in range(2):
-        cols = slice((CHIPS + kind) * HEAD, (CHIPS + kind + 1) * HEAD)
-        for a in range(STEP_ADAPTERS):
-            up_ref[a, :, cols] = kv_ref[2 * a + kind, 0].astype(jnp.float32)
+def widen_kernel(a_hbm, b_hbm, u_hbm, down_hbm, up_hbm, a_ref, b_ref, u_ref, down, up, sems):
+    def fetches(a):
+        return [
+            pltpu.make_async_copy(src.at[:, a], dst.at[:, a], sems.at[n, a])
+            for n, (src, dst) in enumerate([(a_hbm, a_ref), (b_hbm, b_ref), (u_hbm, u_ref)])
+        ]
+
+    pairs = pltpu.make_async_copy(
+        u_hbm.at[:, ADAPTERS], u_ref.at[:, ADAPTERS], sems.at[2, ADAPTERS]
+    )
+    pairs.start()
+    for a in range(ADAPTERS):
+        for copy in fetches(a):
+            copy.start()
+    pairs.wait()
+    stores = []
+    for a in range(ADAPTERS):
+        for copy in fetches(a):
+            copy.wait()
+        for j in range(CHIPS):
+            cols = slice(j * HEAD, (j + 1) * HEAD)
+            down[a, : 2 * RANK, cols] = a_ref[j, a].astype(jnp.float32)
+            down[a, 2 * RANK :, cols] = b_ref[j, a].astype(jnp.float32)
+            up[a, :, cols] = u_ref[j, a].astype(jnp.float32)
+        for kind in range(2):
+            cols = slice((CHIPS + kind) * HEAD, (CHIPS + kind + 1) * HEAD)
+            up[a, :, cols] = u_ref[2 * a + kind, ADAPTERS].astype(jnp.float32)
+        for n, (src, dst) in enumerate([(down, down_hbm), (up, up_hbm)]):
+            stores.append(pltpu.make_async_copy(src.at[a], dst.at[a], sems.at[3 + n, a]))
+            stores[-1].start()
+    for copy in stores:
+        copy.wait()
 
 
 def hbm():
@@ -531,11 +571,14 @@
             jax.ShapeDtypeStruct((CHIPS, ADAPTERS, RANK, HEAD), bf16),
             jax.ShapeDtypeStruct((CHIPS, ADAPTERS + 1, RANK, HEAD), bf16),
         ),
-        in_specs=[smem(), hbm(), hbm(), hbm(), vmem(), hbm(), hbm()],
+        in_specs=[hbm()] * 7,
         out_specs=(hbm(), hbm(), hbm()),
         scratch_shapes=[
+            SMEM((MEMBERS,), jnp.int32),
             VMEM(x.shape, bf16), VMEM(base.shape, bf16), VMEM(grad.shape, bf16),
-            VMEM(down.shape, bf16), VMEM(up.shape, bf16), DMA((5,)),
+            VMEM(segments.shape, jnp.int32),
+            VMEM(down.shape, bf16), VMEM(up.shape, bf16),
+            VMEM((BLOCKS, 2 * BLOCK, BLOCK), f32), DMA((7,)),
             VMEM((BLOCKS, rows, BLOCK), bf16),
             VMEM((N_TENSOR, rows, BLOCK), bf16),
             VMEM((BLOCKS, rows, BLOCK), bf16),
@@ -543,10 +586,9 @@
             VMEM((RANK, cols), bf16),
             VMEM((tokens, HEAD), bf16),
             VMEM((tokens, HEAD), bf16),
-            VMEM((2, HEADS * BLOCK, HEAD), bf16),
             VMEM((BLOCKS, HEADS * BLOCK, HEAD), bf16),
+            VMEM((HEADS * HEAD, tokens), bf16),
             VMEM((BLOCKS, rows, BLOCK), bf16),
-            VMEM((RANK, HEADS * HEAD), f32),
             VMEM((CHIPS, 2 * RANK, HEAD), bf16),
             VMEM((BLOCKS, N_TENSOR, rows, BLOCK), bf16),
             DMA((BLOCKS, 7)), DMA((BLOCKS, 7)),
@@ -570,24 +612,21 @@
 
     return pl.pallas_call(
         widen_kernel,
-        grid=(ADAPTERS // STEP_ADAPTERS,),
         out_shape=(
             jax.ShapeDtypeStruct((ADAPTERS, rows, width), f32),
             jax.ShapeDtypeStruct((ADAPTERS, RANK, cols), f32),
         ),
-        in_specs=[
-            pl.BlockSpec((CHIPS, STEP_ADAPTERS, 2 * RANK, HEAD), lambda a: (0, a, 0, 0)),
-            pl.BlockSpec((CHIPS, STEP_ADAPTERS, RANK, HEAD), lambda a: (0, a, 0, 0)),
-            pl.BlockSpec((CHIPS, STEP_ADAPTERS, RANK, HEAD), lambda a: (0, a, 0, 0)),
-            pl.BlockSpec((2 * STEP_ADAPTERS, 1, RANK, HEAD), lambda a: (a, ADAPTERS, 0, 0)),
+        in_specs=[hbm()] * 3,
+        out_specs=(hbm(), hbm()),
+        scratch_shapes=[
+            VMEM(out_a.shape, bf16), VMEM(out_b.shape, bf16), VMEM(out_u.shape, bf16),
+            VMEM((ADAPTERS, rows, width), f32),
+            VMEM((ADAPTERS, RANK, cols), f32),
+            DMA((5, ADAPTERS + 1)),
         ],
-        out_specs=(
-            pl.BlockSpec((STEP_ADAPTERS, rows, width), lambda a: (a, 0, 0)),
-            pl.BlockSpec((STEP_ADAPTERS, RANK, cols), lambda a: (a, 0, 0)),
-        ),
         compiler_params=pltpu.CompilerParams(vmem_limit_bytes=limit),
         name="widen",
-    )(out_a, out_b, out_u, out_u)
+    )(out_a, out_b, out_u)
 
 
 def solution(mesh):

time: 66.5 us -> 64.8 us (0.974)
  Pallas kernels: 65.7 us -> 63.8 us
    pallas_call x1, Pallas kernels: 62.2 us -> 60.4 us  [per_device(): pl.pallas_call(fused_kernel, out_shape=(jax.ShapeDtypeStruct((CHIPS, ADAP...]
where the time goes in v4:
time: 64.8 us; the launch traced here: 64.5 us
  Pallas kernels  63.8 us (98%)
    pallas_call x1, Pallas kernels, per_device(): pl.pallas_call(fused_kernel, out_shape=(jax.ShapeDtypeStruct((CHIPS, ADAP...  60.4 us
    pallas_call x1, Pallas kernels, per_device(): pl.pallas_call(widen_kernel, out_shape=(jax.ShapeDtypeStruct((ADAPTERS, r...  3.43 us

profile of v4, /device:TPU:1, one launch (start us, length us, event | category | flops | bytes accessed | tf_op | source)
XLA Modules:
  0.0 64.5 jit_solution(3755899208439118652)
XLA Ops:
  0.6 60.4 %fused.1 = (bf16[16,8,32,128]{3,2,1,0:T(8,128)(2,1)}, bf16[16,8,16,128]{3,2,1,0:T(8,128)(2,1)}, bf16[16,9,16,128]{3,2,1,0:T(8,128)(2,1)}) custom-call(s32[32]{0:T(128)} %bitcast.1, bf16[512,2048]{1,0:T(8,128)(2,1)} %x_hbm.1, bf16[512,2304]{1,0:T(8,128)(2,1)} %base_hbm.1, bf16[512,2048]{1,0:T(8,128)(2,1)} %grad_hbm.1, s32[1,512]{1,0:T(1,128)} %seg_hbm.1, ...), custom_call_target="tpu_custom_call" | custom-call | tf_op jit(solution)/shard_map/fused/pallas_call | solution.py:567
  61.0 3.4 %widen.1 = (f32[8,48,2048]{2,1,0:T(8,128)}, f32[8,16,2304]{2,1,0:T(8,128)}) custom-call(bf16[16,8,32,128]{3,2,1,0:T(8,128)(2,1)} %get-tuple-element.5.a_hbm, bf16[16,8,16,128]{3,2,1,0:T(8,128)(2,1)} %get-tuple-element.6.b_hbm, bf16[16,9,16,128]{3,2,1,0:T(8,128)(2,1)} %get-tuple-element.7.u_hbm), custom_call_target="tpu_custom_call" | custom-call | tf_op jit(solution)/shard_map/widen/pallas_call | solution.py:613

commit v5 on v4

--- a/solution.py
+++ b/solution.py
@@ -45,24 +45,31 @@
     return pl.BlockSpec(memory_space=SMEM)
 
 
+FAR_FIRST = ((1, 2), (1, 1), (1, 3), (1, 0), (0, 2), (0, 1), (0, 3))
+
+
+def tensor_peers():
+    me = lax.axis_index("tensor")
+    x, high = me % N_X, me // N_X
+    return [((high + dh) % 2) * N_X + (x + dx) % N_X for dh, dx in FAR_FIRST]
+
+
 def greet_tensor(barrier):
-    dp, me = lax.axis_index("dp"), lax.axis_index("tensor")
-    for d in range(1, N_TENSOR):
-        other = (me + d) % N_TENSOR
+    dp = lax.axis_index("dp")
+    for other in tensor_peers():
         pl.semaphore_signal(barrier, inc=1, device_id=(dp, other), device_id_type=MESH)
 
 
 def tensor_scatter(part, inbox, send, recv):
     dp, me = lax.axis_index("dp"), lax.axis_index("tensor")
     copies = []
-    for d in range(1, N_TENSOR):
-        other = (me + d) % N_TENSOR
+    for n, other in enumerate(tensor_peers()):
         copies.append(
             pltpu.make_async_remote_copy(
                 src_ref=part.at[other % N_X],
                 dst_ref=inbox.at[me],
-                send_sem=send.at[d - 1],
-                recv_sem=recv.at[d - 1],
+                send_sem=send.at[n],
+                recv_sem=recv.at[n],
                 device_id=(dp, other),
                 device_id_type=MESH,
             )
@@ -267,14 +274,14 @@
 def share(part, inbox, send, recv):
     dp, me = lax.axis_index("dp"), lax.axis_index("tensor")
     copies = []
-    for d in range(1, N_TENSOR):
+    for n, other in enumerate(tensor_peers()):
         copies.append(
             pltpu.make_async_remote_copy(
                 src_ref=part,
                 dst_ref=inbox.at[me],
-                send_sem=send.at[d - 1],
-                recv_sem=recv.at[d - 1],
-                device_id=(dp, (me + d) % N_TENSOR),
+                send_sem=send.at[n],
+                recv_sem=recv.at[n],
+                device_id=(dp, other),
                 device_id_type=MESH,
             )
         )
@@ -520,25 +527,9 @@
     scatter_sent(down_b, in_b, 1, sb, rb)
 
 
-def widen_kernel(a_hbm, b_hbm, u_hbm, down_hbm, up_hbm, a_ref, b_ref, u_ref, down, up, sems):
-    def fetches(a):
-        return [
-            pltpu.make_async_copy(src.at[:, a], dst.at[:, a], sems.at[n, a])
-            for n, (src, dst) in enumerate([(a_hbm, a_ref), (b_hbm, b_ref), (u_hbm, u_ref)])
-        ]
-
-    pairs = pltpu.make_async_copy(
-        u_hbm.at[:, ADAPTERS], u_ref.at[:, ADAPTERS], sems.at[2, ADAPTERS]
-    )
-    pairs.start()
-    for a in range(ADAPTERS):
-        for copy in fetches(a):
-            copy.start()
-    pairs.wait()
+def widen_kernel(a_ref, b_ref, u_ref, down_hbm, up_hbm, down, up, sems):
     stores = []
     for a in range(ADAPTERS):
-        for copy in fetches(a):
-            copy.wait()
         for j in range(CHIPS):
             cols = slice(j * HEAD, (j + 1) * HEAD)
             down[a, : 2 * RANK, cols] = a_ref[j, a].astype(jnp.float32)
@@ -548,7 +539,7 @@
             cols = slice((CHIPS + kind) * HEAD, (CHIPS + kind + 1) * HEAD)
             up[a, :, cols] = u_ref[2 * a + kind, ADAPTERS].astype(jnp.float32)
         for n, (src, dst) in enumerate([(down, down_hbm), (up, up_hbm)]):
-            stores.append(pltpu.make_async_copy(src.at[a], dst.at[a], sems.at[3 + n, a]))
+            stores.append(pltpu.make_async_copy(src.at[a], dst.at[a], sems.at[n, a]))
             stores[-1].start()
     for copy in stores:
         copy.wait()
@@ -560,10 +551,15 @@
 
 def per_device(x, base, grad, segments, ids, down, up):
     bf16, f32 = jnp.bfloat16, jnp.float32
+    ids = ids.reshape(-1)
+    x, base, grad, segments, ids, down, up = (
+        pltpu.with_memory_space_constraint(v, pltpu.HBM)
+        for v in (x, base, grad, segments, ids, down, up)
+    )
     tokens, width = x.shape
     cols = base.shape[1]
     rows = KINDS * RANK
-    limit = 58 * 1024 * 1024
+    limit = 40 * 1024 * 1024
     out_a, out_b, out_u = pl.pallas_call(
         fused_kernel,
         out_shape=(
@@ -608,7 +604,7 @@
             collective_id=0, has_side_effects=True, vmem_limit_bytes=limit
         ),
         name="fused",
-    )(ids.reshape(-1), x, base, grad, segments, down, up)
+    )(ids, x, base, grad, segments, down, up)
 
     return pl.pallas_call(
         widen_kernel,
@@ -616,13 +612,12 @@
             jax.ShapeDtypeStruct((ADAPTERS, rows, width), f32),
             jax.ShapeDtypeStruct((ADAPTERS, RANK, cols), f32),
         ),
-        in_specs=[hbm()] * 3,
+        in_specs=[vmem()] * 3,
         out_specs=(hbm(), hbm()),
         scratch_shapes=[
-            VMEM(out_a.shape, bf16), VMEM(out_b.shape, bf16), VMEM(out_u.shape, bf16),
             VMEM((ADAPTERS, rows, width), f32),
             VMEM((ADAPTERS, RANK, cols), f32),
-            DMA((5, ADAPTERS + 1)),
+            DMA((2, ADAPTERS)),
         ],
         compiler_params=pltpu.CompilerParams(vmem_limit_bytes=limit),
         name="widen",

time: 64.8 us -> 63.9 us (0.986)
    pallas_call x1, Pallas kernels: 3.43 us -> 2.21 us  [per_device(): pl.pallas_call(widen_kernel, out_shape=(jax.ShapeDtypeStruct((ADAPTERS, r...]
where the time goes in v5:
time: 63.9 us; the launch traced here: 63.8 us
  Pallas kernels  63.2 us (99%)
  between operations  0.64 us (1%)
    pallas_call x1, Pallas kernels, per_device(): pl.pallas_call(fused_kernel, out_shape=(jax.ShapeDtypeStruct((CHIPS, ADAP...  61 us
    pallas_call x1, Pallas kernels, per_device(): pl.pallas_call(widen_kernel, out_shape=(jax.ShapeDtypeStruct((ADAPTERS, r...  2.21 us

profile of v5, /device:TPU:1, one launch (start us, length us, event | category | flops | bytes accessed | tf_op | source)
XLA Modules:
  0.0 63.8 jit_solution(11054001615655905251)
XLA Ops:
  0.6 61.0 %fused.1 = (bf16[16,8,32,128]{3,2,1,0:T(8,128)(2,1)S(1)}, bf16[16,8,16,128]{3,2,1,0:T(8,128)(2,1)S(1)}, bf16[16,9,16,128]{3,2,1,0:T(8,128)(2,1)S(1)}) custom-call(s32[32]{0:T(128)} %bitcast.1, bf16[512,2048]{1,0:T(8,128)(2,1)} %x_hbm.1, bf16[512,2304]{1,0:T(8,128)(2,1)} %base_hbm.1, bf16[512,2048]{1,0:T(8,128)(2,1)} %grad_hbm.1, s32[1,512]{1,0:T(1,128)} %seg_hbm.1, ...), custom_call_target="tpu_custom_call" | custom-call | tf_op jit(solution)/shard_map/fused/pallas_call | solution.py:563
  61.6 2.2 %widen.1 = (f32[8,48,2048]{2,1,0:T(8,128)}, f32[8,16,2304]{2,1,0:T(8,128)}) custom-call(bf16[16,8,32,128]{3,2,1,0:T(8,128)(2,1)S(1)} %get-tuple-element.5.a_ref, bf16[16,8,16,128]{3,2,1,0:T(8,128)(2,1)S(1)} %get-tuple-element.6.b_ref, bf16[16,9,16,128]{3,2,1,0:T(8,128)(2,1)S(1)} %get-tuple-element.7.u_ref), custom_call_target="tpu_custom_call" | custom-call | tf_op jit(solution)/shard_map/widen/pallas_call | solution.py:609

commit v6 on v5

--- a/solution.py
+++ b/solution.py
@@ -192,7 +192,8 @@
 class Stream:
     def __init__(self, buf, out, owner, sems):
         self.buf, self.out, self.owner = buf, out, owner
-        self.zs, self.zr, self.ys, self.yr, self.cs, self.cr, self.ks = sems
+        self.zs, self.zr, self.ys, self.yr, self.fs, self.fr, self.cs, self.cr, self.ks = sems
+        self.half = buf.shape[1] // 2
         self.tensor = lax.axis_index("tensor")
         self.chip, self.core = split_dp()
         self.y, self.z = self.chip // N_Z, self.chip % N_Z
@@ -233,33 +234,73 @@
         self.twin(n, slot).start()
         pltpu.make_async_copy(self.buf.at[slot], self.out.at[slot], self.ks).start()
 
-    def y_sends(self, dz):
-        for dy in (2, 1, 3):
+    def y_sends(self, dz, steps=(2, 1, 3)):
+        for dy in steps:
             self.y_copy(dz, dy).start()
         self.deliver(dz, self.at(0, -dz))
+
+    def forward(self, k, dz, side):
+        part = pl.ds(0, self.half) if side == 0 else pl.ds(self.half, self.buf.shape[1] - self.half)
+        slot, to = self.at(2 * side - 1, -dz), self.at(1 - 2 * side, 0)
+        return self.forward_copy(k, slot, to, side, part)
+
+    def forwarded(self, k, dz, side):
+        part = pl.ds(0, self.half) if side == 0 else pl.ds(self.half, self.buf.shape[1] - self.half)
+        return self.forward_copy(k, self.at(2, -dz), self.chip, side, part)
+
+    def forward_copy(self, k, slot, to, side, part):
+        return pltpu.make_async_remote_copy(
+            src_ref=self.buf.at[slot, part],
+            dst_ref=self.buf.at[slot, part],
+            send_sem=self.fs.at[2 * k + side],
+            recv_sem=self.fr.at[2 * k + side],
+            device_id=(2 * to + self.owner, self.tensor),
+            device_id_type=MESH,
+        )
 
     def start(self):
         for d in (2, 1, 3):
             self.z_copy(d).start()
-        self.y_sends(0)
+        self.y_sends(0, (1, 3))
+
+    def pass_on(self, k, dz):
+        for side, dy in enumerate((1, 3)):
+            self.y_copy(dz, dy).wait_recv()
+            self.forward(k, dz, side).start()
+            self.deliver(4 + 3 * dz + dy - 1, self.at(-dy, -dz))
 
     def spread(self):
-        for dz in self.nearest_first():
-            self.z_copy(dz).wait_recv()
-            self.y_sends(dz)
+        near, middle, far = self.nearest_first()
+        self.z_copy(near).wait_recv()
+        self.y_sends(near, (1, 3))
+        self.z_copy(middle).wait_recv()
+        self.y_sends(middle)
+        self.pass_on(0, 0)
+        self.z_copy(far).wait_recv()
+        self.y_sends(far)
+        self.pass_on(1, near)
 
     def finish(self):
-        for dz in [0] + self.nearest_first():
+        near, middle, far = self.nearest_first()
+        for dz in (middle, far):
             for dy in (1, 3, 2):
                 self.y_copy(dz, dy).wait_recv()
                 self.deliver(4 + 3 * dz + dy - 1, self.at(-dy, -dz))
+            k, other = (0, 0) if dz is middle else (1, near)
+            for side in range(2):
+                self.forwarded(k, other, side).wait_recv()
+            self.deliver(4 + 3 * other + 1, self.at(2, -other))
 
     def sent(self):
+        near, middle, far = self.nearest_first()
         for d in range(1, N_Z):
             self.z_copy(d).wait_send()
-        for dz in range(N_Z):
-            for dy in range(1, N_Y):
+        for dz, steps in ((0, (1, 3)), (near, (1, 3)), (middle, (1, 2, 3)), (far, (1, 2, 3))):
+            for dy in steps:
                 self.y_copy(dz, dy).wait_send()
+        for k, dz in enumerate((0, near)):
+            for side in range(2):
+                self.forward(k, dz, side).wait_send()
         for n in range(CHIPS):
             self.twin(n, self.chip).wait_send()
         pltpu.make_async_copy(self.buf, self.out, self.ks).wait()
@@ -268,7 +309,7 @@
         arrived(self.out, self.cr)
 
 
-STREAM_SEMS = [DMA((3,)), DMA((3,)), DMA((12,)), DMA((12,)), DMA((CHIPS,)), DMA, DMA]
+STREAM_SEMS = [DMA((3,))] * 2 + [DMA((12,))] * 2 + [DMA((4,))] * 2 + [DMA((CHIPS,)), DMA, DMA]
 
 
 def share(part, inbox, send, recv):
@@ -484,9 +525,9 @@
     own_piece(down_a, in_a, 0, sa, ra)
     own_piece(down_b, in_b, 1, sb, rb)
 
-    stream_a = Stream(buf_a, out_a, 0, sems[0:7])
-    stream_b = Stream(buf_b, out_b, 1, sems[7:14])
-    stream_u = Stream(buf_u, out_u, 1, sems[14:21])
+    stream_a = Stream(buf_a, out_a, 0, sems[0:9])
+    stream_b = Stream(buf_b, out_b, 1, sems[9:18])
+    stream_u = Stream(buf_u, out_u, 1, sems[18:27])
 
     @pl.when(core == 0)
     def _():

time: 63.9 us -> 63.2 us (0.989)
  Pallas kernels: 63.2 us -> 62.5 us
    pallas_call x1, Pallas kernels: 61 us -> 60.3 us  [per_device(): pl.pallas_call(fused_kernel, out_shape=(jax.ShapeDtypeStruct((CHIPS, ADAP...]
where the time goes in v6:
time: 63.2 us; the launch traced here: 63.1 us
  Pallas kernels  62.5 us (99%)
  between operations  0.64 us (1%)
    pallas_call x1, Pallas kernels, per_device(): pl.pallas_call(fused_kernel, out_shape=(jax.ShapeDtypeStruct((CHIPS, ADAP...  60.3 us
    pallas_call x1, Pallas kernels, per_device(): pl.pallas_call(widen_kernel, out_shape=(jax.ShapeDtypeStruct((ADAPTERS, r...  2.21 us

profile of v6, /device:TPU:1, one launch (start us, length us, event | category | flops | bytes accessed | tf_op | source)
XLA Modules:
  0.0 63.1 jit_solution(8636839512372138261)
XLA Ops:
  0.6 60.3 %fused.1 = (bf16[16,8,32,128]{3,2,1,0:T(8,128)(2,1)S(1)}, bf16[16,8,16,128]{3,2,1,0:T(8,128)(2,1)S(1)}, bf16[16,9,16,128]{3,2,1,0:T(8,128)(2,1)S(1)}) custom-call(s32[32]{0:T(128)} %bitcast.1, bf16[512,2048]{1,0:T(8,128)(2,1)} %x_hbm.1, bf16[512,2304]{1,0:T(8,128)(2,1)} %base_hbm.1, bf16[512,2048]{1,0:T(8,128)(2,1)} %grad_hbm.1, s32[1,512]{1,0:T(1,128)} %seg_hbm.1, ...), custom_call_target="tpu_custom_call" | custom-call | tf_op jit(solution)/shard_map/fused/pallas_call | solution.py:604
  60.9 2.2 %widen.1 = (f32[8,48,2048]{2,1,0:T(8,128)}, f32[8,16,2304]{2,1,0:T(8,128)}) custom-call(bf16[16,8,32,128]{3,2,1,0:T(8,128)(2,1)S(1)} %get-tuple-element.5.a_ref, bf16[16,8,16,128]{3,2,1,0:T(8,128)(2,1)S(1)} %get-tuple-element.6.b_ref, bf16[16,9,16,128]{3,2,1,0:T(8,128)(2,1)S(1)} %get-tuple-element.7.u_ref), custom_call_target="tpu_custom_call" | custom-call | tf_op jit(solution)/shard_map/widen/pallas_call | solution.py:650

commit v7 on v6

--- a/solution.py
+++ b/solution.py
@@ -437,12 +437,13 @@
         pltpu.make_async_copy(src, dst, loads.at[n])
         for n, (src, dst) in enumerate(
             [
-                (ids_hbm, ids), (down_hbm, down_ref), (x_hbm, x_ref), (up_hbm, up_ref),
+                (ids_hbm, ids), (down_hbm, down_ref), (x_hbm.at[: 2 * BLOCK], x_ref.at[: 2 * BLOCK]), (up_hbm, up_ref),
                 (grad_hbm, grad), (base_hbm, base), (seg_hbm, seg),
             ]
         )
     ]
-    for copy in fetch:
+    rest = pltpu.make_async_copy(x_hbm.at[2 * BLOCK :], x_ref.at[2 * BLOCK :], loads.at[7])
+    for copy in fetch[:3] + [rest] + fetch[3:]:
         copy.start()
 
     barrier = pltpu.get_barrier_semaphore()
@@ -459,9 +460,13 @@
     adapter = ids[dp]
     fetch[1].wait()
     fetch[2].wait()
-    partial_low = matmul(down_ref[adapter], x_ref[...], NT)
-    for b in range(BLOCKS):
-        part[b] = partial_low[:, b * BLOCK : (b + 1) * BLOCK].astype(bf16)
+    for half in range(2):
+        if half:
+            rest.wait()
+        rows = slice(2 * half * BLOCK, 2 * (half + 1) * BLOCK)
+        partial_low = matmul(down_ref[adapter], x_ref[rows], NT)
+        for b in range(2):
+            part[2 * half + b] = partial_low[:, b * BLOCK : (b + 1) * BLOCK].astype(bf16)
     pl.semaphore_wait(barrier, N_TENSOR - 1 + MEMBERS - 1)
     copies = tensor_scatter(part, inbox, s1, r1)
     fetch[3].wait()
@@ -615,7 +620,7 @@
             VMEM(x.shape, bf16), VMEM(base.shape, bf16), VMEM(grad.shape, bf16),
             VMEM(segments.shape, jnp.int32),
             VMEM(down.shape, bf16), VMEM(up.shape, bf16),
-            VMEM((BLOCKS, 2 * BLOCK, BLOCK), f32), DMA((7,)),
+            VMEM((BLOCKS, 2 * BLOCK, BLOCK), f32), DMA((8,)),
             VMEM((BLOCKS, rows, BLOCK), bf16),
             VMEM((N_TENSOR, rows, BLOCK), bf16),
             VMEM((BLOCKS, rows, BLOCK), bf16),

time: 63.2 us -> 62.9 us (level)
  no operation moved by 1% of the time
where the time goes in v7:
time: 62.9 us; the launch traced here: 62.8 us
  Pallas kernels  62.1 us (99%)
  between operations  0.64 us (1%)
    pallas_call x1, Pallas kernels, per_device(): pl.pallas_call(fused_kernel, out_shape=(jax.ShapeDtypeStruct((CHIPS, ADAP...  59.9 us
    pallas_call x1, Pallas kernels, per_device(): pl.pallas_call(widen_kernel, out_shape=(jax.ShapeDtypeStruct((ADAPTERS, r...  2.21 us

profile of v7, /device:TPU:1, one launch (start us, length us, event | category | flops | bytes accessed | tf_op | source)
XLA Modules:
  0.0 62.8 jit_solution(17303037284910210285)
XLA Ops:
  0.6 59.9 %fused.1 = (bf16[16,8,32,128]{3,2,1,0:T(8,128)(2,1)S(1)}, bf16[16,8,16,128]{3,2,1,0:T(8,128)(2,1)S(1)}, bf16[16,9,16,128]{3,2,1,0:T(8,128)(2,1)S(1)}) custom-call(s32[32]{0:T(128)} %bitcast.1, bf16[512,2048]{1,0:T(8,128)(2,1)} %x_hbm.1, bf16[512,2304]{1,0:T(8,128)(2,1)} %base_hbm.1, bf16[512,2048]{1,0:T(8,128)(2,1)} %grad_hbm.1, s32[1,512]{1,0:T(1,128)} %seg_hbm.1, ...), custom_call_target="tpu_custom_call" | custom-call | tf_op jit(solution)/shard_map/fused/pallas_call | solution.py:609
  60.6 2.2 %widen.1 = (f32[8,48,2048]{2,1,0:T(8,128)}, f32[8,16,2304]{2,1,0:T(8,128)}) custom-call(bf16[16,8,32,128]{3,2,1,0:T(8,128)(2,1)S(1)} %get-tuple-element.5.a_ref, bf16[16,8,16,128]{3,2,1,0:T(8,128)(2,1)S(1)} %get-tuple-element.6.b_ref, bf16[16,9,16,128]{3,2,1,0:T(8,128)(2,1)S(1)} %get-tuple-element.7.u_ref), custom_call_target="tpu_custom_call" | custom-call | tf_op jit(solution)/shard_map/widen/pallas_call | solution.py:655
